TPU v7x, 32 devices: a whole 2x2x4 slice. The times are simulated.
32 devices in a mesh: wide: 8 (over z, core), narrow: 4 (over y, x).
Axes of the slice: x: 2, y: 2, z: 4, core: 2. Of those that a mesh axis runs over, the one named last changes fastest.
Arguments:
- tokens: bfloat16 [32768, 768], P(('wide', 'narrow')), may hold values from -6 to 6
- segment_ids: int32 [32768], P(('wide', 'narrow')), may hold values from -1 to 7, as said below
- out_grad: bfloat16 [32768, 768], P(('wide', 'narrow')), may hold values from -6 to 6
- first_gain: bfloat16 [768], P('narrow'), may hold values from 0.099609375 to 1.8984375
- first_shift: bfloat16 [768], P('narrow'), may hold values from -3 to 3
- query_weight: bfloat16 [768, 768], P('narrow'), may hold values from -0.21875 to 0.21875
- query_bias: bfloat16 [768], P('narrow'), may hold values from -3 to 3
- key_weight: bfloat16 [768, 768], P('narrow'), may hold values from -0.21875 to 0.21875
- value_weight: bfloat16 [768, 768], P('narrow'), may hold values from -0.21875 to 0.21875
- value_bias: bfloat16 [768], P('narrow'), may hold values from -3 to 3
- output_weight: bfloat16 [768, 768], P('narrow'), may hold values from -1.25 to 1.25
- output_bias: bfloat16 [768], P('narrow'), may hold values from -3 to 3
- second_gain: bfloat16 [768], P('narrow'), may hold values from 0.099609375 to 1.8984375
- second_shift: bfloat16 [768], P('narrow'), may hold values from -3 to 3
- up_weight: bfloat16 [768, 3072], P('narrow'), may hold values from -0.21875 to 0.21875
- up_bias: bfloat16 [3072], P('narrow'), may hold values from -3 to 3
- down_weight: bfloat16 [3072, 768], P('narrow'), may hold values from -0.109375 to 0.109375
- down_bias: bfloat16 [768], P('narrow'), may hold values from -3 to 3
Outputs:
- layer_out: bfloat16 [32768, 768], P(('wide', 'narrow'))
- input_grad: bfloat16 [32768, 768], P(('wide', 'narrow'))
- first_gain_grad: float32 [768], P('narrow')
- first_shift_grad: float32 [768], P('narrow')
- query_weight_grad: float32 [768, 768], P('narrow')
- query_bias_grad: float32 [768], P('narrow')
- key_weight_grad: float32 [768, 768], P('narrow')
- value_weight_grad: float32 [768, 768], P('narrow')
- value_bias_grad: float32 [768], P('narrow')
- output_weight_grad: float32 [768, 768], P('narrow')
- output_bias_grad: float32 [768], P('narrow')
- second_gain_grad: float32 [768], P('narrow')
- second_shift_grad: float32 [768], P('narrow')
- up_weight_grad: float32 [768, 3072], P('narrow')
- up_bias_grad: float32 [3072], P('narrow')
- down_weight_grad: float32 [3072, 768], P('narrow')
- down_bias_grad: float32 [768], P('narrow')
Inputs may be any that keep to these rules, and one draw needn't show every extreme that they name: `segment_ids`: within each sequence of 512 rows the segment numbers start at 0 and never fall until the padding rows at its end, marked -1; every sequence has 1 to 128 padding rows.
All inputs are finite; a program needn't handle non-finite values.
Results may differ from a plain program's by a relative error of at most 0.019.
Values may be sent and summed in bfloat16 or wider, within the bound.
No kernel may reach another device: no remote copies, remote signals or barrier semaphores. Data moves between devices by JAX's collectives and lax.ppermute only.
A program may use at most 192 MiB of HBM per device.

v0:
```python
import jax
import jax.numpy as jnp
from jax import lax
from jax.sharding import PartitionSpec as P

D = 768
HEADS = 12
HEAD = 64
LEN = 512


EPSILON = 1e-06


def normalize(v, gain, shift):
    center = v - jnp.mean(v, -1, keepdims=True)
    spread = jnp.mean(center * center, -1, keepdims=True)
    return center * lax.rsqrt(spread + EPSILON) * gain + shift


def product(left, right):
    return jnp.dot(left, right, preferred_element_type=jnp.float32)


def left_product(left, right):
    return jnp.einsum("ti,to->io", left, right, preferred_element_type=jnp.float32)


def right_product(left, right):
    return jnp.einsum("to,io->ti", left, right, preferred_element_type=jnp.float32)


def column_sums(values):
    return jnp.sum(values.astype(jnp.float32), 0)


def masked_scores(qsplit, ksplit, seqsegs):
    raw = jnp.einsum("qhe,khe->hqk", qsplit, ksplit, preferred_element_type=jnp.float32) * HEAD ** (
        -0.5
    )
    same = seqsegs[None, :, None] == seqsegs[None, None, :]
    return jnp.where(same, raw, -1e30)


def attention_forward(item):
    queries, keys, values, seqsegs = item
    qsplit = queries.reshape(LEN, HEADS, HEAD)
    ksplit = keys.reshape(LEN, HEADS, HEAD)
    vsplit = values.reshape(LEN, HEADS, HEAD)
    raw = masked_scores(qsplit, ksplit, seqsegs)
    top = jnp.max(raw, -1, keepdims=True)
    expo = jnp.exp(raw - top)
    total = jnp.sum(expo, -1, keepdims=True)
    probs = (expo / total).astype(jnp.bfloat16)
    result = jnp.einsum("hqk,khe->qhe", probs, vsplit, preferred_element_type=jnp.float32)
    return (result.reshape(LEN, D).astype(jnp.bfloat16), top + jnp.log(total))


def attention_backward(item):
    queries, keys, values, grad_out, logsum, seqsegs = item
    qsplit = queries.reshape(LEN, HEADS, HEAD)
    ksplit = keys.reshape(LEN, HEADS, HEAD)
    vsplit = values.reshape(LEN, HEADS, HEAD)
    gsplit = grad_out.reshape(LEN, HEADS, HEAD)
    probs = jnp.exp(masked_scores(qsplit, ksplit, seqsegs) - logsum)
    grad_probs = jnp.einsum("qhe,khe->hqk", gsplit, vsplit, preferred_element_type=jnp.float32)
    inner = jnp.sum(probs * grad_probs, -1, keepdims=True)
    grad_scores = (probs * (grad_probs - inner)).astype(jnp.bfloat16)
    grad_values = jnp.einsum(
        "hqk,qhe->khe", probs.astype(jnp.bfloat16), gsplit, preferred_element_type=jnp.float32
    )
    grad_queries = jnp.einsum(
        "hqk,khe->qhe", grad_scores, ksplit, preferred_element_type=jnp.float32
    ) * HEAD ** (-0.5)
    grad_keys = jnp.einsum(
        "hqk,qhe->khe", grad_scores, qsplit, preferred_element_type=jnp.float32
    ) * HEAD ** (-0.5)
    return (
        grad_queries.reshape(LEN, D).astype(jnp.bfloat16),
        grad_keys.reshape(LEN, D).astype(jnp.bfloat16),
        grad_values.reshape(LEN, D).astype(jnp.bfloat16),
    )


def shards(
    tokens,
    segment_ids,
    out_grad,
    first_gain,
    first_shift,
    query_weight,
    query_bias,
    key_weight,
    value_weight,
    value_bias,
    output_weight,
    output_bias,
    second_gain,
    second_shift,
    up_weight,
    up_bias,
    down_weight,
    down_bias,
):
    gathered = (
        lax.all_gather(first_gain, "narrow", axis=0, tiled=True),
        lax.all_gather(first_shift, "narrow", axis=0, tiled=True),
        lax.all_gather(query_weight, "narrow", axis=0, tiled=True),
        lax.all_gather(query_bias, "narrow", axis=0, tiled=True),
        lax.all_gather(key_weight, "narrow", axis=0, tiled=True),
        lax.all_gather(value_weight, "narrow", axis=0, tiled=True),
        lax.all_gather(value_bias, "narrow", axis=0, tiled=True),
        lax.all_gather(output_weight, "narrow", axis=0, tiled=True),
        lax.all_gather(output_bias, "narrow", axis=0, tiled=True),
        lax.all_gather(second_gain, "narrow", axis=0, tiled=True),
        lax.all_gather(second_shift, "narrow", axis=0, tiled=True),
        lax.all_gather(up_weight, "narrow", axis=0, tiled=True),
        lax.all_gather(up_bias, "narrow", axis=0, tiled=True),
        lax.all_gather(down_weight, "narrow", axis=0, tiled=True),
        lax.all_gather(down_bias, "narrow", axis=0, tiled=True),
    )
    (
        gain_one,
        shift_one,
        w_query,
        b_query,
        w_key,
        w_value,
        b_value,
        w_output,
        b_output,
        gain_two,
        shift_two,
        w_up,
        b_up,
        w_down,
        b_down,
    ) = gathered
    gain_one = gain_one.astype(jnp.float32)
    shift_one = shift_one.astype(jnp.float32)
    gain_two = gain_two.astype(jnp.float32)
    shift_two = shift_two.astype(jnp.float32)
    rows = tokens.shape[0]
    count = rows // LEN
    seqsegs = segment_ids.reshape(count, LEN)
    inputs = tokens.astype(jnp.float32)
    first_normed = normalize(inputs, gain_one, shift_one).astype(jnp.bfloat16)
    queries = (product(first_normed, w_query) + b_query.astype(jnp.float32)).astype(jnp.bfloat16)
    keys = product(first_normed, w_key).astype(jnp.bfloat16)
    values = (product(first_normed, w_value) + b_value.astype(jnp.float32)).astype(jnp.bfloat16)
    attended, logsum = lax.map(
        attention_forward,
        (
            queries.reshape(count, LEN, D),
            keys.reshape(count, LEN, D),
            values.reshape(count, LEN, D),
            seqsegs,
        ),
    )
    attended = attended.reshape(rows, D)
    middle = inputs + product(attended, w_output) + b_output.astype(jnp.float32)
    second_normed = normalize(middle, gain_two, shift_two).astype(jnp.bfloat16)
    pre = product(second_normed, w_up) + b_up.astype(jnp.float32)
    hidden = jax.nn.gelu(pre, approximate=False).astype(jnp.bfloat16)
    layer_out = (middle + product(hidden, w_down) + b_down.astype(jnp.float32)).astype(jnp.bfloat16)
    again = (
        lax.all_gather(query_weight, "narrow", axis=0, tiled=True),
        lax.all_gather(key_weight, "narrow", axis=0, tiled=True),
        lax.all_gather(value_weight, "narrow", axis=0, tiled=True),
        lax.all_gather(output_weight, "narrow", axis=0, tiled=True),
        lax.all_gather(up_weight, "narrow", axis=0, tiled=True),
        lax.all_gather(down_weight, "narrow", axis=0, tiled=True),
    )
    w_query, w_key, w_value, w_output, w_up, w_down = again
    live = (segment_ids >= 0).astype(jnp.float32)[:, None]
    grad_out = out_grad.astype(jnp.float32) * live
    grad_branch = grad_out.astype(jnp.bfloat16)
    down_bias_grad = column_sums(grad_branch)
    down_weight_grad = left_product(hidden, grad_branch)
    grad_hidden = right_product(grad_branch, w_down)
    unused, gelu_pull = jax.vjp(lambda z: jax.nn.gelu(z, approximate=False), pre)
    grad_pre = gelu_pull(grad_hidden)[0].astype(jnp.bfloat16)
    up_bias_grad = column_sums(grad_pre)
    up_weight_grad = left_product(second_normed, grad_pre)
    grad_second = right_product(grad_pre, w_up)
    unused, second_pull = jax.vjp(normalize, middle, gain_two, shift_two)
    grad_mid_norm, second_gain_grad, second_shift_grad = second_pull(grad_second)
    grad_mid = grad_out + grad_mid_norm
    grad_attn = grad_mid.astype(jnp.bfloat16)
    output_bias_grad = column_sums(grad_attn)
    output_weight_grad = left_product(attended, grad_attn)
    grad_attended = right_product(grad_attn, w_output).astype(jnp.bfloat16)
    grad_queries, grad_keys, grad_values = lax.map(
        attention_backward,
        (
            queries.reshape(count, LEN, D),
            keys.reshape(count, LEN, D),
            values.reshape(count, LEN, D),
            grad_attended.reshape(count, LEN, D),
            logsum,
            seqsegs,
        ),
    )
    grad_queries = grad_queries.reshape(rows, D)
    grad_keys = grad_keys.reshape(rows, D)
    grad_values = grad_values.reshape(rows, D)
    query_bias_grad = column_sums(grad_queries)
    value_bias_grad = column_sums(grad_values)
    query_weight_grad = left_product(first_normed, grad_queries)
    key_weight_grad = left_product(first_normed, grad_keys)
    value_weight_grad = left_product(first_normed, grad_values)
    grad_first = (
        right_product(grad_queries, w_query)
        + right_product(grad_keys, w_key)
        + right_product(grad_values, w_value)
    )
    unused, first_pull = jax.vjp(normalize, inputs, gain_one, shift_one)
    grad_in_norm, first_gain_grad, first_shift_grad = first_pull(grad_first)
    input_grad = (grad_mid + grad_in_norm).astype(jnp.bfloat16)
    shares = (
        lax.psum_scatter(
            first_gain_grad.astype(jnp.bfloat16), "narrow", scatter_dimension=0, tiled=True
        ).astype(jnp.float32),
        lax.psum_scatter(
            first_shift_grad.astype(jnp.bfloat16), "narrow", scatter_dimension=0, tiled=True
        ).astype(jnp.float32),
        lax.psum_scatter(
            query_weight_grad.astype(jnp.bfloat16), "narrow", scatter_dimension=0, tiled=True
        ).astype(jnp.float32),
        lax.psum_scatter(
            query_bias_grad.astype(jnp.bfloat16), "narrow", scatter_dimension=0, tiled=True
        ).astype(jnp.float32),
        lax.psum_scatter(
            key_weight_grad.astype(jnp.bfloat16), "narrow", scatter_dimension=0, tiled=True
        ).astype(jnp.float32),
        lax.psum_scatter(
            value_weight_grad.astype(jnp.bfloat16), "narrow", scatter_dimension=0, tiled=True
        ).astype(jnp.float32),
        lax.psum_scatter(
            value_bias_grad.astype(jnp.bfloat16), "narrow", scatter_dimension=0, tiled=True
        ).astype(jnp.float32),
        lax.psum_scatter(
            output_weight_grad.astype(jnp.bfloat16), "narrow", scatter_dimension=0, tiled=True
        ).astype(jnp.float32),
        lax.psum_scatter(
            output_bias_grad.astype(jnp.bfloat16), "narrow", scatter_dimension=0, tiled=True
        ).astype(jnp.float32),
        lax.psum_scatter(
            second_gain_grad.astype(jnp.bfloat16), "narrow", scatter_dimension=0, tiled=True
        ).astype(jnp.float32),
        lax.psum_scatter(
            second_shift_grad.astype(jnp.bfloat16), "narrow", scatter_dimension=0, tiled=True
        ).astype(jnp.float32),
        lax.psum_scatter(
            up_weight_grad.astype(jnp.bfloat16), "narrow", scatter_dimension=0, tiled=True
        ).astype(jnp.float32),
        lax.psum_scatter(
            up_bias_grad.astype(jnp.bfloat16), "narrow", scatter_dimension=0, tiled=True
        ).astype(jnp.float32),
        lax.psum_scatter(
            down_weight_grad.astype(jnp.bfloat16), "narrow", scatter_dimension=0, tiled=True
        ).astype(jnp.float32),
        lax.psum_scatter(
            down_bias_grad.astype(jnp.bfloat16), "narrow", scatter_dimension=0, tiled=True
        ).astype(jnp.float32),
    )
    summed = (
        lax.psum(shares[0].astype(jnp.bfloat16), "wide").astype(jnp.float32),
        lax.psum(shares[1].astype(jnp.bfloat16), "wide").astype(jnp.float32),
        lax.psum(shares[2].astype(jnp.bfloat16), "wide").astype(jnp.float32),
        lax.psum(shares[3].astype(jnp.bfloat16), "wide").astype(jnp.float32),
        lax.psum(shares[4].astype(jnp.bfloat16), "wide").astype(jnp.float32),
        lax.psum(shares[5].astype(jnp.bfloat16), "wide").astype(jnp.float32),
        lax.psum(shares[6].astype(jnp.bfloat16), "wide").astype(jnp.float32),
        lax.psum(shares[7].astype(jnp.bfloat16), "wide").astype(jnp.float32),
        lax.psum(shares[8].astype(jnp.bfloat16), "wide").astype(jnp.float32),
        lax.psum(shares[9].astype(jnp.bfloat16), "wide").astype(jnp.float32),
        lax.psum(shares[10].astype(jnp.bfloat16), "wide").astype(jnp.float32),
        lax.psum(shares[11].astype(jnp.bfloat16), "wide").astype(jnp.float32),
        lax.psum(shares[12].astype(jnp.bfloat16), "wide").astype(jnp.float32),
        lax.psum(shares[13].astype(jnp.bfloat16), "wide").astype(jnp.float32),
        lax.psum(shares[14].astype(jnp.bfloat16), "wide").astype(jnp.float32),
    )
    return (
        layer_out,
        input_grad,
        summed[0],
        summed[1],
        summed[2],
        summed[3],
        summed[4],
        summed[5],
        summed[6],
        summed[7],
        summed[8],
        summed[9],
        summed[10],
        summed[11],
        summed[12],
        summed[13],
        summed[14],
    )


def solution(mesh):
    in_specs = (
        P(("wide", "narrow"), None),
        P(("wide", "narrow")),
        P(("wide", "narrow"), None),
        P("narrow"),
        P("narrow"),
        P("narrow", None),
        P("narrow"),
        P("narrow", None),
        P("narrow", None),
        P("narrow"),
        P("narrow", None),
        P("narrow"),
        P("narrow"),
        P("narrow"),
        P("narrow", None),
        P("narrow"),
        P("narrow", None),
        P("narrow"),
    )
    out_specs = (
        P(("wide", "narrow"), None),
        P(("wide", "narrow"), None),
        P("narrow"),
        P("narrow"),
        P("narrow", None),
        P("narrow"),
        P("narrow", None),
        P("narrow", None),
        P("narrow"),
        P("narrow", None),
        P("narrow"),
        P("narrow"),
        P("narrow"),
        P("narrow", None),
        P("narrow"),
        P("narrow", None),
        P("narrow"),
    )
    return jax.shard_map(shards, mesh=mesh, in_specs=in_specs, out_specs=out_specs, check_vma=False)
```

profile of v0, /device:TPU:0, one launch (start us, length us, event | category | flops | bytes accessed | tf_op | source)
XLA Modules:
  0.0 707.3 jit_solution(5255935174280605779)
XLA Ops:
  14.8 17.7 %all-reduce.20 = (bf16[768]{0:T(1024)(128)(2,1)S(1)}, bf16[768]{0:T(1024)(128)(2,1)S(1)}, bf16[768]{0:T(1024)(128)(2,1)S(1)}, bf16[768]{0:T(1024)(128)(2,1)S(1)}...) all-reduce(bf16[768]{0:T(1024)(128)(2,1)S(1)} %dynamic-update-slice, ...), channel_id=1, replica_groups=mesh['wide'=8,'narrow'=4] {'narrow'}, use_global_device_ids=true, to_apply=%add.2 | all-reduce | flops 5376 | bytes 21504
  36.9 7.2 %all-gather = bf16[4,1,768]{2,1,0:T(2,128)(2,1)S(1)} all-gather(bf16[1,1,768]{2,1,0:T(2,128)(2,1)S(1)} %reshape.343), channel_id=1, replica_groups=mesh['wide'=8,'narrow'=4] {'narrow'}, dimensions={0}, use_global_device_ids=true | all-gather | bytes 7680 | tf_op jit(solution)/shard_map/all_gather | solution.py:118
  54.0 16.2 %all-gather.8.cloned.1.call-done = bf16[768,768]{1,0:T(8,128)(2,1)} async-done(((bf16[192,768]{1,0:T(8,128)(2,1)}), bf16[768,768]{1,0:T(8,128)(2,1)}) %all-gather.8.cloned.1.call-update) | async-done | bytes 1179664 | tf_op jit(solution)/shard_map/all_gather | solution.py:111
  76.8 22.9 %all-gather.12.cloned.1.call-done = bf16[768,768]{1,0:T(8,128)(2,1)} async-done(((bf16[192,768]{1,0:T(8,128)(2,1)}), bf16[768,768]{1,0:T(8,128)(2,1)}) %all-gather.12.cloned.1.call-update) | async-done | bytes 1179664 | tf_op jit(solution)/shard_map/all_gather | solution.py:110
  107.7 26.3 %while.26 = (s32[]{:T(128)}, bf16[2,512,768]{2,1,0:T(8,128)(2,1)}, f32[2,12,512,1]{2,1,3,0:T(8,128)}, bf16[2,512,768]{1,2,0:T(8,128)(2,1)}, s32[2,512]{1,0:T(2,1...) while((s32[]{:T(128)}, bf16[2,512,768]{2,1,0:T(8,128)(2,1)}, ...), condition=%wide.region_5.6_spmd, body=%wide.region_2.5_spmd.sunk | while | flops 843704320 | bytes 50019424 | solution.py:151
  139.5 48.4 %all-gather.16.cloned.1.call-done = bf16[768,3072]{1,0:T(8,128)(2,1)} async-done(((bf16[192,3072]{1,0:T(8,128)(2,1)}), bf16[768,3072]{1,0:T(8,128)(2,1)}) %all-gather.16.cloned.1.call-update) | async-done | bytes 4718608 | tf_op jit(solution)/shard_map/all_gather | solution.py:117
  188.0 38.1 %multiply_convert_fusion.3 = (bf16[1024,3072]{1,0:T(8,128)(2,1)}, f32[1024,3072]{1,0:T(8,128)}, f32[1024,3072]{1,0:T(8,128)}) fusion(f32[3072]{0:T(1024)S(1)} %bitcast.158, bf16[768,3072]{1,0:T(8,128)(2,1)} %all-gather.16.cloned.1.call-done, f32[1024,768]{0,1:T(8,128)} %copy-done.4, f32[768]{0:T(1024)S(1)} %copy-done.57, f32[768]{0:T(1024)S(1)} %copy-done.45, ...), kind=kOutput, calls=%fused_computation.40 | convolution fusion | flops 5043388416 | bytes 39348224 | tf_op jit(solution)/shard_map/dot_general | solution.py:22
  226.1 20.7 %all-gather.18.cloned.1.call-done = bf16[3072,768]{1,0:T(8,128)(2,1)} async-done(((bf16[768,768]{1,0:T(8,128)(2,1)}), bf16[3072,768]{1,0:T(8,128)(2,1)}) %all-gather.18.cloned.1.call-update) | async-done | bytes 4718608 | tf_op jit(solution)/shard_map/all_gather | solution.py:119
  246.8 17.9 %fusion.56 = (bf16[3072]{0:T(1024)(128)(2,1)}, bf16[1024,3072]{1,0:T(8,128)(2,1)}) fusion(f32[1024,3072]{1,0:T(8,128)} %get-tuple-element.293, bf16[3072,768]{1,0:T(8,128)(2,1)} %all-gather.18.cloned.1.call-done, bf16[1024,768]{0,1:T(8,128)(2,1)S(1)} %copy-done.9, f32[1024]{0:T(1024)S(1)} %copy-done.41, f32[1024,3072]{1,0:T(8,128)} %get-tuple-element.307, ...), kind=kOutput, calls=%fused_computation.112 | convolution fusion | flops 4884526080 | bytes 37771264 | tf_op jit(solution)/shard_map/to,io->ti/dot_general | solution.py:30
  264.7 10.3 %fusion.55 = (bf16[768]{0:T(1024)(128)(2,1)}, f32[1024,768]{1,0:T(8,128)}) fusion(bf16[1024,3072]{1,0:T(8,128)(2,1)} %get-tuple-element.312, bf16[768,3072]{1,0:T(8,128)(2,1)} %all-gather.16.cloned.1.call-done), kind=kOutput, calls=%fused_computation.111 | convolution fusion | flops 4832623616 | bytes 14157312 | tf_op jit(solution)/shard_map/to,io->ti/dot_general | solution.py:30
  292.1 94.3 %while.27 = (s32[]{:T(128)}, bf16[2,512,768]{1,2,0:T(8,128)(2,1)}, bf16[2,512,768]{2,1,0:T(8,128)(2,1)}, bf16[2,512,768]{1,2,0:T(8,128)(2,1)}, bf16[2,512,768]{1...) while((s32[]{:T(128)}, bf16[2,512,768]{1,2,0:T(8,128)(2,1)}, ...), condition=%wide.region_12.13_spmd, body=%wide.region_10.12_spmd.sunk | while | flops 2062673920 | bytes 212220912 | solution.py:193
  302.9 11.1 %multiply_reduce_fusion.5 = (f32[12,512]{1,0:T(8,128)S(1)}, f32[12,512,512]{1,2,0:T(8,128)}) fusion(f32[12,512,512]{1,2,0:T(8,128)} %fusion.132, f32[12,512]{1,0:T(8,128)S(1)} %dynamic-slice_bitcast_fusion.2, pred[512,512]{0,1:T(8,128)(4,1)S(1)} %broadcast_compare_fusion.5, bf16[512,12,64]{0,2,1:T(8,128)(2,1)S(1)} %bitcast.135, ...), kind=kOutput, calls=%fused_computation.17.clone.1 | convolution fusion | flops 418375680 | bytes 27049984 | tf_op jit(solution)/shard_map/while/body/eval_jaxpr/qhe,khe->hqk/dot_general | solution.py:66
  315.7 7.0 multiply_convert_fusion.7
  330.5 6.5 fusion.133
  350.1 11.0 %multiply_reduce_fusion.5 = (f32[12,512]{1,0:T(8,128)S(1)}, f32[12,512,512]{1,2,0:T(8,128)}) fusion(f32[12,512,512]{1,2,0:T(8,128)} %fusion.132, f32[12,512]{1,0:T(8,128)S(1)} %dynamic-slice_bitcast_fusion.2, pred[512,512]{0,1:T(8,128)(4,1)S(1)} %broadcast_compare_fusion.5, bf16[512,12,64]{0,2,1:T(8,128)(2,1)S(1)} %bitcast.135, ...), kind=kOutput, calls=%fused_computation.17.clone.1 | convolution fusion | flops 418375680 | bytes 27049984 | tf_op jit(solution)/shard_map/while/body/eval_jaxpr/qhe,khe->hqk/dot_general | solution.py:66
  362.7 7.0 multiply_convert_fusion.7
  400.0 10.0 %convolution_convert_fusion.1 = bf16[768,3072]{1,0:T(8,128)(2,1)} fusion(bf16[1024,3072]{1,0:T(8,128)(2,1)} %get-tuple-element.312, f32[1024,768]{0,1:T(8,128)} %copy-done.4, f32[768]{0:T(1024)S(1)} %copy-done.58, f32[768]{0:T(1024)S(1)} %copy-done.46, f32[1024]{0:T(1024)S(1)} %copy-done.48, f32[1024]{0:T(1024)S(1)} %copy-done.36), kind=kOutput, calls=%fused_computation.55 | convolution fusion | flops 4838129664 | bytes 14170112 | tf_op jit(solution)/shard_map/ti,to->io/dot_general | solution.py:26
  411.4 10.0 %convolution_convert_fusion = bf16[3072,768]{1,0:T(8,128)(2,1)} fusion(bf16[1024,3072]{1,0:T(8,128)(2,1)} %get-tuple-element.292, bf16[1024,768]{0,1:T(8,128)(2,1)S(1)} %copy-done.11, f32[1024]{0:T(1024)S(1)} %copy-done.42), kind=kOutput, calls=%fused_computation.54 | convolution fusion | flops 4836556800 | bytes 12587008 | tf_op jit(solution)/shard_map/ti,to->io/dot_general | solution.py:26
  436.7 15.5 %all-reduce.19 = (bf16[768]{0:T(1024)(128)(2,1)S(1)}, bf16[768]{0:T(1024)(128)(2,1)S(1)}, bf16[768]{0:T(1024)(128)(2,1)S(1)}, bf16[768]{0:T(1024)(128)(2,1)S(1)}...) all-reduce(bf16[768]{0:T(1024)(128)(2,1)S(1)} %dynamic-update-slice, ...), channel_id=1, replica_groups=mesh['wide'=8,'narrow'=4] {'narrow'}, use_global_device_ids=true, to_apply=%add.7 | all-reduce | flops 9984 | bytes 39936
  452.8 13.8 %all-reduce.17 = (bf16[192]{0:T(256)(128)(2,1)S(1)}, bf16[192]{0:T(256)(128)(2,1)S(1)}, bf16[192]{0:T(256)(128)(2,1)S(1)}, bf16[192]{0:T(256)(128)(2,1)S(1)}, bf...) all-reduce(bf16[192]{0:T(256)(128)(2,1)S(1)} %dynamic-slice.9, ...), channel_id=1, replica_groups=mesh['wide'=8,'narrow'=4] {'wide'}, use_global_device_ids=true, to_apply=%region_17.18 | all-reduce | flops 2304 | bytes 9216 | tf_op jit(solution)/shard_map/psum | solution.py:268
  483.3 60.1 %reduce-scatter.15.cloned.1.call-done = bf16[192,3072]{1,0:T(8,128)(2,1)} async-done(((bf16[768,3072]{1,0:T(8,128)(2,1)}), bf16[192,3072]{1,0:T(8,128)(2,1)}) %reduce-scatter.15.cloned.1.call-update) | async-done | bytes 1179664 | tf_op jit(solution)/shard_map/reduce_scatter | solution.py:254
  543.4 60.0 %reduce-scatter.17.cloned.1.call-done = bf16[768,768]{1,0:T(8,128)(2,1)} async-done(((bf16[3072,768]{1,0:T(8,128)(2,1)}), bf16[768,768]{1,0:T(8,128)(2,1)}) %reduce-scatter.17.cloned.1.call-update) | async-done | bytes 1179664 | tf_op jit(solution)/shard_map/reduce_scatter | solution.py:260
  603.4 9.5 %add_convert_fusion.2 = bf16[1024,768]{0,1:T(8,128)(2,1)} fusion(f32[1024,768]{0,1:T(8,128)S(1)} %copy-done.6, bf16[1024,3072]{1,0:T(8,128)(2,1)} %get-tuple-element.292, bf16[3072,768]{1,0:T(8,128)(2,1)} %all-gather.18.cloned.1.call-done, f32[768]{0:T(1024)S(1)} %convert_element_type.275), kind=kOutput, calls=%fused_computation.80 | convolution fusion | flops 4834197504 | bytes 15731712 | tf_op jit(solution)/shard_map/dot_general | solution.py:22
  615.5 76.8 %all-reduce.23.cloned.1.call-done = (bf16[192,768]{1,0:T(8,128)(2,1)}, bf16[192,768]{1,0:T(8,128)(2,1)}, bf16[192,768]{1,0:T(8,128)(2,1)}, bf16[192,768]{1,0:T(8...) async-done(((bf16[192,768]{1,0:T(8,128)(2,1)}, bf16[192,768]{1,0:T(8,128)(2,1)}, bf16[192,768]{1,0:T(8,128)(2,1)}, bf16[192,768]{1,0:T(8,128)(2,1)}, ...) | async-done | bytes 3538960 | tf_op jit(solution)/shard_map/psum | solution.py:270
  (357 shorter events, 191.8 us)
Async XLA Ops:
  7.3 40.0 %all-gather.10.cloned.1.call-start = ((), (), s32[]{:S(2)}) async-start(), calls=%async_computation.7 | async-start | bytes 1474560 | tf_op jit(solution)/shard_map/all_gather | solution.py:108
  8.0 62.1 %all-gather.8.cloned.1.call-start = ((), (), s32[]{:S(2)}) async-start(), calls=%async_computation.6 | async-start | bytes 1474560 | tf_op jit(solution)/shard_map/all_gather | solution.py:111
  8.8 91.0 %all-gather.12.cloned.1.call-start = ((), (), s32[]{:S(2)}) async-start(), calls=%async_computation.8 | async-start | bytes 1474560 | tf_op jit(solution)/shard_map/all_gather | solution.py:110
  9.5 124.5 %all-gather.14.cloned.1.call-start = ((), (), s32[]{:S(2)}) async-start(), calls=%async_computation.9 | async-start | bytes 1474560 | tf_op jit(solution)/shard_map/all_gather | solution.py:113
  10.1 177.9 %all-gather.16.cloned.1.call-start = ((), (), s32[]{:S(2)}) async-start(), calls=%async_computation.10 | async-start | bytes 5898240 | tf_op jit(solution)/shard_map/all_gather | solution.py:117
  10.7 236.1 %all-gather.18.cloned.1.call-start = ((), (), s32[]{:S(2)}) async-start(), calls=%async_computation.11 | async-start | bytes 5898240 | tf_op jit(solution)/shard_map/all_gather | solution.py:119
  11.2 468.8 %reduce-scatter.13.cloned.1.call-start = ((), (), s32[]{:S(2)}) async-start(), calls=%async_computation.15 | async-start | bytes 1474560 | tf_op jit(solution)/shard_map/reduce_scatter | solution.py:242
  32.5 67.2 %copy-start.33 = (f32[768]{0:T(1024)}, f32[768]{0:T(1024)S(1)}, u32[]{:S(2)}) copy-start(f32[768]{0:T(1024)S(1)} %convert_element_type.261) | copy-start | bytes 9220
  32.5 67.2 %copy-start.55 = (f32[768]{0:T(1024)}, f32[768]{0:T(1024)S(1)}, u32[]{:S(2)}) copy-start(f32[768]{0:T(1024)S(1)} %convert_element_type.262) | copy-start | bytes 9220
  34.3 99.8 %copy-start.1 = (bf16[1024,768]{0,1:T(8,128)(2,1)}, bf16[1024,768]{0,1:T(8,128)(2,1)S(1)}, u32[]{:S(2)}) copy-start(bf16[1024,768]{0,1:T(8,128)(2,1)S(1)} %copy.85) | copy-start | bytes 4718596
  34.6 65.2 %copy-start.29 = (f32[1024]{0:T(1024)}, f32[1024]{0:T(1024)S(1)}, u32[]{:S(2)}) copy-start(f32[1024]{0:T(1024)S(1)} %broadcast_multiply_fusion.1) | copy-start | bytes 12292
  35.0 64.7 %copy-start.37 = (f32[1024]{0:T(1024)}, f32[1024]{0:T(1024)S(1)}, u32[]{:S(2)}) copy-start(f32[1024]{0:T(1024)S(1)} %fusion.39) | copy-start | bytes 12292
  137.5 50.5 %copy-start.45 = (f32[768]{0:T(1024)S(1)}, f32[768]{0:T(1024)}, u32[]{:S(2)}) copy-start(f32[768]{0:T(1024)} %convert_element_type.270) | copy-start | bytes 9220
  137.5 144.8 %copy-start.35 = (f32[1024]{0:T(1024)}, f32[1024]{0:T(1024)S(1)}, u32[]{:S(2)}) copy-start(f32[1024]{0:T(1024)S(1)} %broadcast_multiply_fusion) | copy-start | bytes 12292
  139.5 142.7 %copy-start.47 = (f32[1024]{0:T(1024)}, f32[1024]{0:T(1024)S(1)}, u32[]{:S(2)}) copy-start(f32[1024]{0:T(1024)S(1)} %fusion.40) | copy-start | bytes 12292
  188.0 58.8 %copy-start.9 = (bf16[1024,768]{0,1:T(8,128)(2,1)S(1)}, bf16[1024,768]{0,1:T(8,128)(2,1)}, u32[]{:S(2)}) copy-start(bf16[1024,768]{0,1:T(8,128)(2,1)} %copy.91) | copy-start | bytes 4718596
  188.0 58.8 %copy-start.41 = (f32[1024]{0:T(1024)S(1)}, f32[1024]{0:T(1024)}, u32[]{:S(2)}) copy-start(f32[1024]{0:T(1024)} %compare_convert_fusion) | copy-start | bytes 12292
  288.2 191.9 %reduce-scatter.11.cloned.1.call-start = ((), (), s32[]{:S(2)}) async-start(), calls=%async_computation.14 | async-start | bytes 1474560 | tf_op jit(solution)/shard_map/reduce_scatter | solution.py:236
  391.0 89.1 %reduce-scatter.7.cloned.1.call-start = ((), (), s32[]{:S(2)}) async-start(), calls=%async_computation.12 | async-start | bytes 1474560 | tf_op jit(solution)/shard_map/reduce_scatter | solution.py:227
  395.6 87.7 %reduce-scatter.9.cloned.1.call-start = ((), (), s32[]{:S(2)}) async-start(), calls=%async_computation.13 | async-start | bytes 1474560 | tf_op jit(solution)/shard_map/reduce_scatter | solution.py:233
  399.9 143.5 %reduce-scatter.15.cloned.1.call-start = ((), (), s32[]{:S(2)}) async-start(), calls=%async_computation.16 | async-start | bytes 5898240 | tf_op jit(solution)/shard_map/reduce_scatter | solution.py:254
  410.0 193.4 %reduce-scatter.17.cloned.1.call-start = ((), (), s32[]{:S(2)}) async-start(), calls=%async_computation.17 | async-start | bytes 5898240 | tf_op jit(solution)/shard_map/reduce_scatter | solution.py:260
  421.4 270.9 %all-reduce.23.cloned.1.call-start = ((), (), s32[]{:S(2)}) async-start(), calls=%async_computation.18 | async-start | bytes 7077888 | tf_op jit(solution)/shard_map/psum | solution.py:270
  477.3 126.1 %copy-start.6 = (f32[1024,768]{0,1:T(8,128)S(1)}, f32[1024,768]{0,1:T(8,128)}, u32[]{:S(2)}) copy-start(f32[1024,768]{0,1:T(8,128)} %copy-done.4) | copy-start | bytes 9437188
  (77 other events, 485.8 us)
Sparse Core Ops, SparseCore 0:
  10.0 30.5 all-gather.9
  42.4 27.7 all-gather.7
  72.0 27.7 all-gather.11
  101.4 27.7 all-gather.13
  130.9 57.0 all-gather.15
  189.7 57.0 all-gather.17
  288.3 28.5 reduce-scatter.12
  391.1 28.5 reduce-scatter.10
  423.2 28.7 reduce-scatter.6
  454.8 28.4 reduce-scatter.8
  486.3 57.0 reduce-scatter.14
  546.3 57.0 reduce-scatter.16
  606.3 85.9 all-reduce.22
where the time goes:
time: 716 us; the launch traced here: 707 us
  waiting for transfers between devices  312 us (44%)
  matrix products  204 us (28%)
  local copies, waits for them, and re-layouts  64.3 us (9%)
  other arithmetic  54.7 us (8%)
  blocking collectives  54.2 us (8%)
  between operations  17.1 us (2%)
    psum x1, waiting for transfers between devices, shards(): lax.psum(shares[2].astype(jnp.bfloat16), 'wide').astype(jnp.float32)  76.8 us
    dot_general x6, matrix products, product(): return jnp.dot(left, right, preferred_element_type=jnp.float32)  63.3 us
    reduce_scatter x1, waiting for transfers between devices, shards(): lax.psum_scatter(up_weight_grad.astype(jnp.bfloat16), 'narrow', scatter_d...  60.1 us
    reduce_scatter x1, waiting for transfers between devices, shards(): lax.psum_scatter(down_weight_grad.astype(jnp.bfloat16), 'narrow', scatter...  60 us
    all_gather x1, waiting for transfers between devices, shards(): lax.all_gather(up_weight, 'narrow', axis=0, tiled=True)  48.4 us
    dot_general x6, matrix products, right_product(): jnp.einsum('to,io->ti', left, right, preferred_element_type=jnp.float32)  37.5 us
    unnamed x2, blocking collectives  33.2 us
    dot_general x6, matrix products, left_product(): jnp.einsum('ti,to->io', left, right, preferred_element_type=jnp.float32)  31.7 us
  transfers between devices with their start and end apart: 13, of which 8 were waited for; matrix products, arithmetic and copies ran while one was open for 37% of the time, Pallas kernels for 0%

commit v1 on v0

v1 whole, which is shorter than its diff:
```python
import functools

import jax
import jax.numpy as jnp
from jax import lax
from jax.experimental import pallas as pl
from jax.experimental.pallas import tpu as pltpu
from jax.sharding import PartitionSpec as P

D = 768
HEADS = 12
HEAD = 64
LEN = 512
FF = 3072
EPSILON = 1e-06
TILE = 256
BAND = D // 8
PAIR = 2 * HEAD
PAIRS = HEADS // 2
CHUNKS = (4, 2)
LOG2E = 1.4426950408889634
LN2 = 0.6931471805599453

bf16 = jnp.bfloat16
f32 = jnp.float32
NN = (((1,), (0,)), ((), ()))
NT = (((1,), (1,)), ((), ()))
TN = (((0,), (0,)), ((), ()))
ANY = pl.BlockSpec(memory_space=pl.ANY)


def dot(left, right, dims=NN):
    return lax.dot_general(left, right, dims, preferred_element_type=f32)


def shape(dims, kind):
    return jax.ShapeDtypeStruct(dims, kind)


def column_sum(values):
    return jnp.sum(values, 0, keepdims=True)


def whole(dims):
    return pl.BlockSpec(dims, lambda *at: (0,) * len(dims))


def rows_block(dims):
    return pl.BlockSpec(dims, lambda at, *rest: (at,) + (0,) * (len(dims) - 1))


class Order:
    def __init__(self, meta):
        self.meta, self.last = meta, []

    def run(
        self, name, body, ins, in_specs, outs, out_specs, grid, scratch, macs, limit, alias={}
    ):
        moved = sum(a.size * a.dtype.itemsize for a in ins)
        moved += sum(o.size * o.dtype.itemsize for o in outs)
        used, extra = len(ins), len(self.last)

        def inner(meta, *refs):
            body(meta, *refs[:used], *refs[used + extra :])

        ins = [pltpu.with_memory_space_constraint(a, pltpu.HBM) for a in ins]
        outs = [pltpu.HBM(o.shape, o.dtype) for o in outs]
        got = pl.pallas_call(
            inner,
            out_shape=outs,
            grid_spec=pltpu.PrefetchScalarGridSpec(
                num_scalar_prefetch=1,
                grid=grid,
                in_specs=[*in_specs] + [ANY] * extra,
                out_specs=out_specs,
                scratch_shapes=scratch,
            ),
            input_output_aliases=alias,
            compiler_params=pltpu.CompilerParams(vmem_limit_bytes=limit * 2**20),
            cost_estimate=pl.CostEstimate(
                flops=int(2 * macs * 1.5), bytes_accessed=moved, transcendentals=0
            ),
            name=name,
        )(self.meta, *ins, *self.last)
        self.last = [got[0]]
        return got

    def small(self, name, body, ins, outs, meta=False):
        moved = sum(a.size * a.dtype.itemsize for a in [*ins, *outs])
        used, extra = len(ins), len(self.last)
        lead = [self.meta] if meta else []

        def inner(*refs):
            held, refs = refs[: len(lead)], refs[len(lead) :]
            body(*held, *refs[:used], *refs[used + extra :])

        vmem = pl.BlockSpec(memory_space=pltpu.VMEM)
        smem = pl.BlockSpec(memory_space=pltpu.SMEM)
        got = pl.pallas_call(
            inner,
            out_shape=outs,
            in_specs=[smem] * len(lead) + [vmem] * used + [ANY] * extra,
            out_specs=[vmem] * len(outs),
            compiler_params=pltpu.CompilerParams(vmem_limit_bytes=16 * 2**20),
            cost_estimate=pl.CostEstimate(flops=0, bytes_accessed=moved, transcendentals=0),
            name=name,
        )(*lead, *ins, *self.last)
        self.last = [got[0]]
        return got


def fill(meta, pieces, target, sems):
    count = 1 if len(pieces) == 1 else len(pieces)
    half = target.shape[0] // 8
    copies = []
    for i in range(count):
        start = pl.multiple_of(meta[i] * half, half) if count > 1 else 0
        copies.append(
            pltpu.make_async_copy(
                pieces[i], target.at[pl.ds(start, pieces[i].shape[0])], sems.at[i]
            )
        )
    return copies


def first_step(copies):
    @pl.when(pl.program_id(0) == 0)
    def _():
        for copy in copies:
            copy.start()
        for copy in copies:
            copy.wait()


def as_column(row):
    return jnp.broadcast_to(row.astype(f32), (8, row.shape[1])).T[:, :1]


def standard(v):
    center = v - jnp.mean(v, -1, keepdims=True)
    rate = lax.rsqrt(jnp.mean(center * center, -1, keepdims=True) + EPSILON)
    return center * rate, rate


def pack(order, parts):
    width = sum(p.shape[1] for p in parts)

    def body(*refs):
        at = 0
        for src in refs[:-1]:
            refs[-1][:, at : at + src.shape[1]] = src[...]
            at += src.shape[1]

    return order.small("pack", body, parts, [shape((parts[0].shape[0], width), bf16)])[0]


def copies(order, halves, wholes=()):
    ins = [*halves, *wholes]
    dims = [(a.shape[0] // 2, a.shape[1]) for a in halves] + [a.shape for a in wholes]

    def body(meta, *refs):
        for i, (src, dst) in enumerate(zip(refs[: len(ins)], refs[len(ins) :])):
            if i < len(halves):
                half = dst.shape[0]
                dst[...] = src[pl.ds(pl.multiple_of(meta[13] * half, half), half)]
            else:
                dst[...] = src[...]

    return order.small("copies", body, ins, [shape(d, bf16) for d in dims], True)


def sums_of(order, plan):
    ins, where = [], {}
    for _, terms in plan:
        for array, _ in terms:
            if id(array) not in where:
                where[id(array)] = len(ins)
                ins.append(array)

    def body(*refs):
        for (rows, terms), out in zip(plan, refs[len(ins) :]):
            total = None
            for array, start in terms:
                term = refs[where[id(array)]][start : start + rows].astype(f32)
                total = term if total is None else total + term
            out[...] = total.astype(bf16)

    dims = [(rows, terms[0][0].shape[1]) for rows, terms in plan]
    return order.small("sums_of", body, ins, [shape(d, bf16) for d in dims])


def pick(order, own, got):
    def body(meta, own, got, out):
        inner = jnp.full(out.shape, meta[14], jnp.int32) == 1
        out[...] = jnp.where(inner, own[...], got[...])

    return order.small("pick", body, [own, got], [shape(own.shape, bf16)], True)[0]


def finish(order, pairs, plan):
    flat = [a for pair in pairs for a in pair]
    half = flat[0].shape[0]

    def body(meta, *refs):
        core = meta[13]
        for (width, parts), out in zip(plan, refs[len(flat) :]):
            at = 0
            for which, first, cols in parts:
                for i in range(2):
                    place = core if i == 0 else 1 - core
                    rows = pl.ds(pl.multiple_of(place * half, half), half)
                    value = refs[2 * which + i][:, first : first + cols]
                    out[rows, at : at + cols] = value.astype(f32)
                at += cols

    outs = [shape((2 * half, width), f32) for width, _ in plan]
    return order.small("finish", body, flat, outs, True)


def attend(order, tokens, vec, segs, pieces, at_seq, before):
    count = len(pieces)
    rows = tokens.shape[0]
    seqs = rows // LEN
    held = 0 if before is None else len(before)

    def body(meta, tok, vec, seg, *rest):
        pieces, rest = rest[:count], rest[count + held :]
        fn_t, q, k, v, att, att_t, expo, inv, bias, w, sems = rest
        p = pl.program_id(0)

        @pl.when(p == 0)
        def _():
            copies = fill(meta, pieces, w, sems)
            for copy in copies:
                copy.start()
            row = seg[0].astype(f32)
            bias[...] = jnp.where(as_column(row) == row, 0.0, -1e30)
            normed = standard(tok[...].astype(f32))[0] * vec[0:1] + vec[1:2]
            low = normed.astype(bf16)
            fn_t[...] = low.T
            for copy in copies:
                copy.wait()
            q[...] = ((dot(low, w[:, :D]) + vec[2:3]) * (LOG2E * HEAD**-0.5)).astype(bf16)
            k[...] = dot(low, w[:, D : 2 * D]).astype(bf16)
            v[...] = (dot(low, w[:, 2 * D :]) + vec[3:4]).astype(bf16)

        lane = lax.broadcasted_iota(jnp.int32, (LEN, PAIR), 1)
        mine_cols = pl.ds(pl.multiple_of(p * PAIR, PAIR), PAIR)
        vt = v[:, mine_cols].T
        keys = k[:, mine_cols]
        queries = q[:, mine_cols]
        parts = []
        for h in range(2):
            mine = (lane < HEAD) if h == 0 else (lane >= HEAD)
            scores = dot(jnp.where(mine, keys, 0).astype(bf16), queries, NT) + bias[...]
            e = jnp.exp2(scores - jnp.max(scores, 0, keepdims=True))
            rate = 1.0 / jnp.sum(e, 0, keepdims=True)
            low = e.astype(bf16)
            expo[h] = low
            inv[0, h : h + 1] = rate
            parts.append(dot(vt[HEAD * h : HEAD * h + HEAD], low) * rate)
        both = jnp.concatenate(parts, 0)
        att_t[...] = both.astype(bf16)
        att[...] = both.T.astype(bf16)

    seq = pl.BlockSpec((LEN, D), lambda p, m: (at_seq, 0))
    ins = [tokens, vec, segs.reshape(seqs, 1, LEN), *pieces]
    alias = {}
    if before is not None:
        alias = {1 + len(ins) + i: i for i in range(held)}
        ins += before
    return order.run(
        "attend",
        body,
        ins,
        [
            seq,
            whole((8, D)),
            pl.BlockSpec((1, 1, LEN), lambda p, m: (at_seq, 0, 0)),
        ]
        + [ANY] * (count + held),
        [
            shape((D, rows), bf16),
            shape((rows, D), bf16),
            shape((rows, D), bf16),
            shape((rows, D), bf16),
            shape((rows, D), bf16),
            shape((D, rows), bf16),
            shape((seqs * HEADS, LEN, LEN), bf16),
            shape((seqs * PAIRS, 8, LEN), f32),
        ],
        [
            pl.BlockSpec((D, LEN), lambda p, m: (0, at_seq)),
            seq,
            seq,
            seq,
            pl.BlockSpec((LEN, PAIR), lambda p, m: (at_seq, p)),
            pl.BlockSpec((PAIR, LEN), lambda p, m: (p, at_seq)),
            pl.BlockSpec((2, LEN, LEN), lambda p, m: (at_seq * PAIRS + p, 0, 0)),
            pl.BlockSpec((1, 8, LEN), lambda p, m: (at_seq * PAIRS + p, 0, 0)),
        ],
        (PAIRS,),
        [
            pltpu.VMEM((LEN, LEN), f32),
            pltpu.VMEM((D, 3 * D), bf16),
            pltpu.SemaphoreType.DMA((count,)),
        ],
        LEN * D * D * 3 + LEN * LEN * D * 8,
        28,
        alias,
    )


def vectors(order, sources):
    n, share = len(sources), sources[0].shape[1]

    def body(meta, *refs):
        srcs, (vec, ub) = refs[:n], refs[n:]
        rows = []
        for s in range(n):
            total = jnp.zeros((12, share), f32)
            for i in range(n):
                total = jnp.where(meta[15 + i] == s, srcs[i][...].astype(f32), total)
            rows.append(total)
        vec[...] = jnp.concatenate([r[:8] for r in rows], 1)
        ub[...] = jnp.concatenate([r[8 + i : 9 + i] for r in rows for i in range(4)], 1)

    outs = [shape((8, D), f32), shape((1, FF), f32)]
    return order.small("vectors", body, sources, outs, True)


def gelu_both(x):
    size = jnp.abs(x) * 0.7071067811865476
    t = 1.0 / (1.0 + 0.3275911 * size)
    bell = jnp.exp2(x * x * (-0.5 * LOG2E))
    poly = 0.5 * 1.061405429
    for c in (-1.453152027, 1.421413741, -0.284496736, 0.254829592):
        poly = poly * t + 0.5 * c
    tail = poly * t * bell
    cdf = jnp.where(x >= 0, 1.0 - tail, tail)
    return x * cdf, cdf + x * bell * 0.3989422804014327


def feed(order, attended, tokens, out_grad, live, vec, up_bias, pieces):
    count = len(pieces)
    rows = tokens.shape[0]

    def body(meta, att, tok, og, seg, vec, ub, *rest):
        pieces, (mid, sn_t, hid, slope, gb, down_sum, w, sems) = rest[:count], rest[count:]
        first_step(fill(meta, pieces, w, sems))
        m = tok[...].astype(f32) + dot(att[...], w[:, FF:]) + vec[4:5]
        mid[...] = m
        low = (standard(m)[0] * vec[5:6] + vec[6:7]).astype(bf16)
        sn_t[...] = low.T
        grad = jnp.where(as_column(seg[0]) >= 0, og[...].astype(f32), 0.0)
        gb[...] = grad.astype(bf16)

        @pl.when(pl.program_id(0) == 0)
        def _():
            down_sum[...] = jnp.zeros_like(down_sum)

        down_sum[0:1] += column_sum(grad)
        for at in range(0, FF, 512):
            pre = dot(low, w[:, at : at + 512]) + ub[:, at : at + 512]
            act, der = gelu_both(pre)
            hid[:, at : at + 512] = act.astype(bf16)
            slope[:, at : at + 512] = der.astype(bf16)

    blk = rows_block((TILE, D))
    wide = rows_block((TILE, FF))
    return order.run(
        "feed",
        body,
        [attended, tokens, out_grad, live, vec, up_bias, *pieces],
        [blk, blk, blk, rows_block((1, 1, TILE)), whole((8, D)), whole((1, FF))] + [ANY] * count,
        [
            shape((rows, D), f32),
            shape((D, rows), bf16),
            shape((rows, FF), bf16),
            shape((rows, FF), bf16),
            shape((rows, D), bf16),
            shape((8, D), f32),
        ],
        [blk, pl.BlockSpec((D, TILE), lambda at, m: (0, at)), wide, wide, blk, whole((8, D))],
        (rows // TILE,),
        [pltpu.VMEM((D, FF + D), bf16), pltpu.SemaphoreType.DMA((count,))],
        rows * D * (FF + D) * 3,
        32,
    )


def down_out(order, hidden, mid, vec, pieces):
    count = len(pieces)
    rows = hidden.shape[0]

    def body(meta, hid, mid, vec, *rest):
        pieces, (out, w, sems) = rest[:count], rest[count:]
        first_step(fill(meta, pieces, w, sems))
        out[...] = (mid[...] + dot(hid[...], w[...]) + vec[7:8]).astype(bf16)

    blk = rows_block((TILE, D))
    return order.run(
        "down_out",
        body,
        [hidden, mid, vec, *pieces],
        [rows_block((TILE, FF)), blk, whole((8, D))] + [ANY] * count,
        [shape((rows, D), bf16)],
        [blk],
        (rows // TILE,),
        [pltpu.VMEM((FF, D), bf16), pltpu.SemaphoreType.DMA((count,))],
        rows * D * FF,
        24,
    )[0]


def normal_grad(grad, gain, hat, rate):
    inner = grad * gain
    return rate * (
        inner
        - jnp.mean(inner, -1, keepdims=True)
        - hat * jnp.mean(inner * hat, -1, keepdims=True)
    )


def back(order, slope, mid, gb, vec, downs, pieces):
    nd, count = len(downs), len(pieces)
    rows = gb.shape[0]

    def body(meta, slope, mid, gb, vec, *rest):
        downs, pieces, rest = rest[:nd], rest[nd : nd + count], rest[nd + count :]
        gpre, gmid, gattn, gatt, sums, up_sum, wd, w, sems_d, sems = rest
        first_step(fill(meta, downs, wd, sems_d) + fill(meta, pieces, w, sems))

        @pl.when(pl.program_id(0) == 0)
        def _():
            sums[...] = jnp.zeros_like(sums)
            up_sum[...] = jnp.zeros_like(up_sum)

        grad = None
        for at in range(0, FF, 512):
            cols = slice(at, at + 512)
            low = (dot(gb[...], wd[cols], NT) * slope[:, cols].astype(f32)).astype(bf16)
            gpre[:, cols] = low
            up_sum[0:1, cols] += column_sum(low.astype(f32))
            term = dot(low, w[:, cols], NT)
            grad = term if grad is None else grad + term
        hat, rate = standard(mid[...])
        sums[0:1] += column_sum(grad * hat)
        sums[1:2] += column_sum(grad)
        g = gb[...].astype(f32) + normal_grad(grad, vec[5:6], hat, rate)
        gmid[...] = g
        low = g.astype(bf16)
        gattn[...] = low
        sums[2:3] += column_sum(low.astype(f32))
        gatt[...] = dot(low, w[:, FF:], NT).astype(bf16)

    blk = rows_block((TILE, D))
    wide = rows_block((TILE, FF))
    return order.run(
        "back",
        body,
        [slope, mid, gb, vec, *downs, *pieces],
        [wide, blk, blk, whole((8, D))] + [ANY] * (nd + count),
        [
            shape((rows, FF), bf16),
            shape((rows, D), f32),
            shape((rows, D), bf16),
            shape((rows, D), bf16),
            shape((8, D), f32),
            shape((8, FF), f32),
        ],
        [wide, blk, blk, blk, whole((8, D)), whole((8, FF))],
        (rows // TILE,),
        [
            pltpu.VMEM((FF, D), bf16),
            pltpu.VMEM((D, FF + D), bf16),
            pltpu.SemaphoreType.DMA((nd,)),
            pltpu.SemaphoreType.DMA((count,)),
        ],
        rows * D * (2 * FF + D),
        32,
    )


def attend_back(order, fn_t, q, k, v, att_t, gatt, expo, inv, first, pairs):
    rows = q.shape[0]
    count = rows // LEN
    width = PAIR * pairs

    def body(meta, q, k, v, att_t, g, expo, inv, fn_t, *rest):
        dq, dk, dv, send, own, near, far, sums, grads, held, sems = rest
        s, p = pl.program_id(0), pl.program_id(1)

        def moves():
            return [
                pltpu.make_async_copy(
                    fn_t.at[pl.ds(pl.multiple_of(meta[5 + j] * BAND, BAND), BAND)],
                    held.at[pl.ds(j * BAND, BAND)],
                    sems.at[j],
                )
                for j in range(8)
            ]

        @pl.when((s == 0) & (p == 0))
        def _():
            for copy in moves():
                copy.start()

        queries, values = q[...], v[...]
        kt = k[...].T
        gt = g[...].astype(f32).T
        both = att_t[...].astype(f32) * gt
        parts, dks, dvs = [], [], []
        for h in range(2):
            at = slice(HEAD * h, HEAD * h + HEAD)
            rate = inv[0, h : h + 1]
            delta = jnp.sum(both[at], 0, keepdims=True) * rate
            scaled = (gt[at] * rate).astype(bf16)
            e = expo[h]
            ds = (e.astype(f32) * (dot(values[:, at], scaled) - delta)).astype(bf16)
            parts.append(dot(kt[at], ds))
            dvs.append(dot(e, scaled, NT))
            dks.append(dot(ds, queries[:, at]) * LN2)
        three = (
            (jnp.concatenate(parts, 0).T * HEAD**-0.5).astype(bf16),
            jnp.concatenate(dks, 1).astype(bf16),
            jnp.concatenate(dvs, 1).astype(bf16),
        )
        mine = pl.ds(pl.multiple_of(s * LEN, LEN), LEN)
        for i, (ref, value) in enumerate(zip((dq, dk, dv), three)):
            ref[...] = value
            grads[mine, pl.ds(pl.multiple_of(i * width + p * PAIR, PAIR), PAIR)] = value

        @pl.when((s == count - 1) & (p == pairs - 1))
        def _():
            for copy in moves():
                copy.wait()
            right = grads[...]
            send[...] = dot(held[: 4 * BAND], right).astype(bf16)
            kept = dot(held[4 * BAND :], right).astype(bf16)
            own[...] = kept[:BAND]
            near[...] = kept[BAND : 2 * BAND]
            far[...] = kept[2 * BAND :]
            sums[...] = jnp.broadcast_to(column_sum(right.astype(f32)), sums.shape)

    blk = pl.BlockSpec((LEN, PAIR), lambda s, p, m: (s, p + first))
    out = pl.BlockSpec((LEN, PAIR), lambda s, p, m: (s, p))
    widths = [4 * BAND, BAND, BAND, 2 * BAND]
    return order.run(
        "attend_back",
        body,
        [q, k, v, att_t, gatt, expo, inv, fn_t],
        [blk] * 3
        + [
            pl.BlockSpec((PAIR, LEN), lambda s, p, m: (p + first, s)),
            blk,
            pl.BlockSpec((2, LEN, LEN), lambda s, p, m: (s * PAIRS + p + first, 0, 0)),
            pl.BlockSpec((1, 8, LEN), lambda s, p, m: (s * PAIRS + p + first, 0, 0)),
            ANY,
        ],
        [shape((rows, width), bf16)] * 3
        + [shape((n, 3 * width), bf16) for n in widths]
        + [shape((8, 3 * width), f32)],
        [out] * 3 + [whole((n, 3 * width)) for n in widths] + [whole((8, 3 * width))],
        (count, pairs),
        [
            pltpu.VMEM((rows, 3 * width), bf16),
            pltpu.VMEM((D, rows), bf16),
            pltpu.SemaphoreType.DMA((8,)),
        ],
        rows * LEN * PAIR * pairs * 9 + rows * D * 3 * width,
        28,
    )


def grad_first(order, dqkv, tokens, gmid, vec, pieces):
    count = len(pieces)
    rows = tokens.shape[0]
    flat = [t for chunk in dqkv for t in chunk]
    starts = [0]
    for chunk in dqkv:
        starts.append(starts[-1] + chunk[0].shape[1])

    def body(meta, tok, gmid, vec, *rest):
        grads, rest = rest[: len(flat)], rest[len(flat) :]
        pieces, (out, sums, w, sems) = rest[:count], rest[count:]
        first_step(fill(meta, pieces, w, sems))

        @pl.when(pl.program_id(0) == 0)
        def _():
            sums[...] = jnp.zeros_like(sums)

        total = None
        for i, ref in enumerate(grads):
            at = (i % 3) * D + starts[i // 3]
            term = dot(ref[...], w[:, at : at + ref.shape[1]], NT)
            total = term if total is None else total + term
        hat, rate = standard(tok[...].astype(f32))
        sums[0:1] += column_sum(total * hat)
        sums[1:2] += column_sum(total)
        out[...] = (gmid[...] + normal_grad(total, vec[0:1], hat, rate)).astype(bf16)

    blk = rows_block((TILE, D))
    return order.run(
        "grad_first",
        body,
        [tokens, gmid, vec, *flat, *pieces],
        [blk, blk, whole((8, D))] + [rows_block((TILE, t.shape[1])) for t in flat] + [ANY] * count,
        [shape((rows, D), bf16), shape((8, D), f32)],
        [blk, whole((8, D))],
        (rows // TILE,),
        [pltpu.VMEM((D, 3 * D), bf16), pltpu.SemaphoreType.DMA((count,))],
        rows * D * D * 3,
        24,
    )


def down_grad(order, hidden, gb):
    rows = gb.shape[0]
    band = FF // 8

    def body(meta, hid, gb, send, own, near, far):
        low = dot(hid[...], gb[...], TN).astype(bf16)
        at = pl.program_id(0)

        @pl.when(at < 4)
        def _():
            send[...] = low

        @pl.when(at == 4)
        def _():
            own[...] = low

        @pl.when(at == 5)
        def _():
            near[...] = low

        @pl.when(at >= 6)
        def _():
            far[...] = low

    return order.run(
        "down_grad",
        body,
        [hidden, gb],
        [pl.BlockSpec((rows, band), lambda j, m: (0, m[5 + j])), whole((rows, D))],
        [shape((n * band, D), bf16) for n in (4, 1, 1, 2)],
        [
            pl.BlockSpec((band, D), lambda j, m: (jnp.minimum(j, 3), 0)),
            whole((band, D)),
            whole((band, D)),
            pl.BlockSpec((band, D), lambda j, m: (jnp.maximum(j - 6, 0), 0)),
        ],
        (8,),
        [],
        rows * D * FF,
        24,
    )


def weight_grad(name, order, left, first, recv):
    rows = left[0][0].shape[1]
    width = min(r.shape[1] for _, rights in left for r in rights)
    width = min(width, D)
    plan = []
    flat = []
    for i, (_, rights) in enumerate(left):
        for r in rights:
            for at in range(r.shape[1] // width):
                plan.append((i, len(flat), at))
            flat.append(r)
    steps = len(plan)
    nl, nr = len(left), len(flat)
    total = steps * width

    def body(meta, *rest):
        lefts, rights, rest = rest[:nl], rest[nl : nl + nr], rest[nl + nr :]
        got = None
        if recv is not None:
            got, rest = rest[0], rest[1:]
        nout = 1 if recv is None else 3
        outs, rest = rest[:nout], rest[nout:]
        held, sems = rest
        step = pl.program_id(0)

        @pl.when(step == 0)
        def _():
            copies = []
            for i in range(nl):
                for j in range(4):
                    start = pl.multiple_of(meta[first + j] * BAND, BAND)
                    copies.append(
                        pltpu.make_async_copy(
                            lefts[i].at[pl.ds(start, BAND)],
                            held.at[i, pl.ds(j * BAND, BAND)],
                            sems.at[i * 4 + j],
                        )
                    )
            for copy in copies:
                copy.start()
            for copy in copies:
                copy.wait()

        def emit(which, right):
            value = dot(held[which], right)
            if recv is None:
                outs[0][...] = value.astype(bf16)
                return
            low = (value + got[...].astype(f32)).astype(bf16)
            outs[0][...] = low[:BAND]
            outs[1][...] = low[BAND : 2 * BAND]
            outs[2][...] = low[2 * BAND :]

        begin = 0
        for r in range(nr):
            mine = [s for s, p in enumerate(plan) if p[1] == r]

            @pl.when((step >= mine[0]) & (step <= mine[-1]))
            def _(r=r):
                which = plan[[s for s, p in enumerate(plan) if p[1] == r][0]][0]
                emit(which, rights[r][...])

    def right_spec(r):
        mine = [s for s, p in enumerate(plan) if p[1] == r]
        return pl.BlockSpec((rows, width), lambda s, m: (0, jnp.clip(s - mine[0], 0, len(mine) - 1)))

    cols = lambda n: pl.BlockSpec((n, width), lambda s, m: (0, s))
    ins = [l for l, _ in left] + flat + ([] if recv is None else [recv])
    in_specs = [ANY] * nl + [right_spec(r) for r in range(nr)]
    if recv is None:
        outs, out_specs = [shape((4 * BAND, total), bf16)], [cols(4 * BAND)]
    else:
        in_specs.append(cols(4 * BAND))
        outs = [shape((n * BAND, total), bf16) for n in (1, 1, 2)]
        out_specs = [cols(n * BAND) for n in (1, 1, 2)]
    return order.run(
        name,
        body,
        ins,
        in_specs,
        outs,
        out_specs,
        (steps,),
        [pltpu.VMEM((nl, 4 * BAND, rows), bf16), pltpu.SemaphoreType.DMA((4 * nl,))],
        rows * 4 * BAND * total,
        24,
    )


class Links:
    def __init__(self, mesh):
        self.wide, self.narrow = mesh.shape["wide"], mesh.shape["narrow"]
        self.paired = self.wide == 8 and self.narrow == 4

    def move(self, value, target):
        pairs = []
        for w in range(self.wide):
            for n in range(self.narrow):
                to = target(w, n)
                if to is not None:
                    pairs.append((w * self.narrow + n, to[0] * self.narrow + to[1]))
        return lax.ppermute(value, ("wide", "narrow"), pairs)

    def swap(self, value):
        return self.move(value, lambda w, n: (w ^ 1, n))

    def near(self, value):
        return self.move(value, lambda w, n: (w, n ^ (1 + (w & 1))))

    def far(self, value):
        return self.move(value, lambda w, n: (w, n ^ (2 - (w & 1))))

    def inward(self, value):
        return self.move(value, lambda w, n: {0: (w + 2, n), 3: (w - 2, n)}.get(w >> 1))

    def across(self, value):
        return self.move(value, lambda w, n: {1: (w + 2, n), 2: (w - 2, n)}.get(w >> 1))

    def outward(self, value):
        return self.move(value, lambda w, n: {1: (w - 2, n), 2: (w + 2, n)}.get(w >> 1))

    def along(self, value, step):
        return self.move(value, lambda w, n: (w, n ^ step))

    def level(self, value, step):
        return self.move(value, lambda w, n: (w ^ (2 * step), n))

    def meta(self):
        table = []
        for w in range(self.wide):
            for n in range(self.narrow):
                core, level = w & 1, w >> 1
                a, b, d = n ^ (1 + core), n ^ (2 - core), n ^ 3
                if not self.paired:
                    row = [0] * 5 + list(range(8)) + [0, 0] + list(range(self.narrow))
                else:
                    row = [2 * n, 2 * a, 2 * d + core, 2 * b, 2 * d + 1 - core]
                    row += [2 * s + 1 - core for s in (n, a, b, d)]
                    row += [2 * s + core for s in (n, b, a, d)]
                    row += [core, int(level in (1, 2)), n, n ^ 1, n ^ 2, d]
                table.append(row)
        place = lax.axis_index(("wide", "narrow"))
        return lax.dynamic_index_in_dim(jnp.array(table, jnp.int32), place, keepdims=False)

    def shares(self, packed):
        if not self.paired:
            sources = lax.all_gather(packed, "narrow", axis=0)
            return [sources[i] for i in range(self.narrow)]
        return [packed] + [self.along(packed, i) for i in (1, 2, 3)]

    def sum_all(self, value):
        if not self.paired:
            return lax.psum(value, ("wide", "narrow"))
        value = value + self.swap(value)
        value = value + self.along(value, 1) + self.along(value, 2) + self.along(value, 3)
        return value + self.level(value, 1) + self.level(value, 2) + self.level(value, 3)

    def sum_levels(self, own):
        groups = [list(range(c, self.wide, 2)) for c in range(2)]
        return lax.psum(own, "wide", axis_index_groups=groups)

    def whole_sum(self, sent, kept):
        full = jnp.concatenate([sent, *kept], 0)
        mine = lax.psum_scatter(full, "narrow", scatter_dimension=0, tiled=True)
        mine = lax.psum(mine, "wide")
        half = mine.shape[0] // 2
        return mine[:half], mine[half:]


def layer(links, *args):
    (
        tokens,
        segment_ids,
        out_grad,
        first_gain,
        first_shift,
        query_weight,
        query_bias,
        key_weight,
        value_weight,
        value_bias,
        output_weight,
        output_bias,
        second_gain,
        second_shift,
        up_weight,
        up_bias,
        down_weight,
        down_bias,
    ) = args
    order = Order(links.meta())
    paired = links.paired
    share = first_gain.shape[0]
    gather = lambda v: [lax.all_gather(v, "narrow", axis=0, tiled=True)]
    small = (
        first_gain,
        first_shift,
        query_bias,
        value_bias,
        output_bias,
        second_gain,
        second_shift,
        down_bias,
    )
    live = segment_ids.reshape(-1, 1, TILE)

    pack_one = pack(order, [query_weight, key_weight, value_weight])
    shares = links.shares(jnp.concatenate([*small, up_bias]).reshape(-1, share))
    vec, up_b = vectors(order, shares)
    if paired:
        near_one = links.near(pack_one)
        far_one = links.far(copies(order, [near_one])[0])
        w_one = [pack_one, near_one, far_one, links.swap(near_one), links.swap(far_one)]
    else:
        w_one = gather(pack_one)
    pack_two = pack(order, [up_weight, output_weight])
    kept = attend(order, tokens, vec, segment_ids, w_one, 0, None)
    if paired:
        near_two = links.near(pack_two)
        far_two = links.far(copies(order, [near_two])[0])
        w_two = [pack_two, near_two, far_two, links.swap(near_two), links.swap(far_two)]
    else:
        w_two = gather(pack_two)
    for s in range(1, tokens.shape[0] // LEN):
        kept = attend(order, tokens, vec, segment_ids, w_one, s, list(kept))
    fn_t, q, k, v, att, att_t, expo, inv = kept
    if paired:
        down_half, down_copy = copies(order, [down_weight], [down_weight])
        near_down = links.near(down_copy)
        far_down = links.along(down_half, 3)
        w_down = [down_weight, near_down, far_down, links.swap(near_down), links.swap(far_down)]
    else:
        w_down = gather(down_weight)
    mid, sn_t, hidden, slope, gb, down_sum = feed(
        order, att, tokens, out_grad, live, vec, up_b, w_two
    )

    d_send, d_own, d_near, d_far = down_grad(order, hidden, gb)
    gpre, gmid, gattn, gatt, mid_sums, up_sum = back(order, slope, mid, gb, vec, w_down, w_two)
    lefts = [(sn_t, [gpre]), (att_t, [gattn])]
    if paired:
        high = d_own.shape[0]
        d_got = links.swap(d_send)
        (d_far,) = sums_of(order, [(2 * high, [(d_far, 0), (d_got, 2 * high)])])
        d_got2 = links.near(d_far)
    s_send = weight_grad("second_send", order, lefts, 5, None)[0]
    s_got = links.swap(s_send) if paired else jnp.zeros_like(s_send)

    chunks, first = [], 0
    for c, pairs in enumerate(CHUNKS):
        chunks.append(attend_back(order, fn_t, q, k, v, att_t, gatt, expo, inv, first, pairs))
        first += pairs
        if c == 0:
            if paired:
                c_send, c_own, c_near, c_far = chunks[0][3:7]
                d_near, d_own = sums_of(
                    order,
                    [
                        (high, [(d_near, 0), (d_got, high), (d_got2, high)]),
                        (high, [(d_own, 0), (d_got, 0), (d_got2, 0)]),
                    ],
                )
                d_got3 = links.far(d_near)
                c_got = links.swap(c_send)
            s_own, s_near, s_far = weight_grad("second_keep", order, lefts, 9, s_got)
            if paired:
                s_got2 = links.near(s_far)
                d_own, c_far = sums_of(
                    order,
                    [
                        (high, [(d_own, 0), (d_got3, 0)]),
                        (2 * BAND, [(c_far, 0), (c_got, 2 * BAND)]),
                    ],
                )
                d_got = links.inward(d_own)
                c_got2 = links.near(c_far)
    dqkv = [chunk[:3] for chunk in chunks]
    if paired:
        e_send, e_own, e_near, e_far = chunks[1][3:7]
        e_got = links.swap(e_send)
        s_near, s_own, d_own = sums_of(
            order,
            [
                (BAND, [(s_near, 0), (s_got2, BAND)]),
                (BAND, [(s_own, 0), (s_got2, 0)]),
                (high, [(d_own, 0), (d_got, 0)]),
            ],
        )
        s_got = links.far(s_near)
        d_got = links.across(d_own)
        c_near, c_own, e_far = sums_of(
            order,
            [
                (BAND, [(c_near, 0), (c_got, BAND), (c_got2, BAND)]),
                (BAND, [(c_own, 0), (c_got, 0), (c_got2, 0)]),
                (2 * BAND, [(e_far, 0), (e_got, 2 * BAND)]),
            ],
        )
        c_got = links.far(c_near)
        e_got2 = links.near(e_far)
    input_grad, first_sums = grad_first(order, dqkv, tokens, gmid, vec, w_one)
    cols = lambda c, i: slice(i * PAIR * CHUNKS[c], (i + 1) * PAIR * CHUNKS[c])
    bias = lambda i: jnp.concatenate([chunks[c][7][:1, cols(c, i)] for c in range(2)], 1)
    total = links.sum_all(
        jnp.concatenate(
            [
                first_sums[:2],
                bias(0),
                bias(2),
                mid_sums[2:3],
                mid_sums[:2],
                down_sum[:1],
                up_sum[:1].reshape(4, D),
            ],
            0,
        )
    )
    if paired:
        e_near, e_own, c_own, s_own, d_own = sums_of(
            order,
            [
                (BAND, [(e_near, 0), (e_got, BAND), (e_got2, BAND)]),
                (BAND, [(e_own, 0), (e_got, 0), (e_got2, 0)]),
                (BAND, [(c_own, 0), (c_got, 0)]),
                (BAND, [(s_own, 0), (s_got, 0)]),
                (high, [(d_own, 0), (d_got, 0)]),
            ],
        )
        e_got = links.far(e_near)
        c_got = links.level(c_own, 1)
        s_own = links.sum_levels(s_own)
        d_got = links.outward(d_own)
    layer_out = down_out(order, hidden, mid, vec, w_down)
    if paired:
        e_own, c_own = sums_of(
            order,
            [(BAND, [(e_own, 0), (e_got, 0)]), (BAND, [(c_own, 0), (c_got, 0)])],
        )
        e_got, c_got = links.level(e_own, 1), links.level(c_own, 2)
        d_own = pick(order, d_own, d_got)
        d_pair = (d_own, links.swap(d_own))
        e_own, c_own = sums_of(
            order,
            [(BAND, [(e_own, 0), (e_got, 0)]), (BAND, [(c_own, 0), (c_got, 0)])],
        )
        e_got = links.level(e_own, 2)
        c_pair = (c_own, links.swap(c_own))
        s_pair = (s_own, links.swap(s_own))
        (down_weight_grad,) = finish(order, [d_pair], [(D, [(0, 0, D)])])
        (e_own,) = sums_of(order, [(BAND, [(e_own, 0), (e_got, 0)])])
        e_pair = (e_own, links.swap(e_own))
    else:
        d_pair = links.whole_sum(d_send, (d_own, d_near, d_far))
        s_pair = links.whole_sum(s_send, (s_own, s_near, s_far))
        c_pair, e_pair = [links.whole_sum(c[3], c[4:7]) for c in chunks]
        (down_weight_grad,) = finish(order, [d_pair], [(D, [(0, 0, D)])])
    first_grads = finish(
        order,
        [c_pair, e_pair],
        [(D, [(c, cols(c, i).start, PAIR * CHUNKS[c]) for c in range(2)]) for i in range(3)],
    )
    up_weight_grad, output_weight_grad = finish(
        order, [s_pair], [(FF, [(0, 0, FF)]), (D, [(0, FF, D)])]
    )

    n = lax.axis_index("narrow")
    mine = lax.dynamic_slice_in_dim(total[:8], n * share, share, 1)
    up_share = up_bias.shape[0]
    up_mine = lax.dynamic_slice_in_dim(total[8:].reshape(FF), n * up_share, up_share)
    return (
        layer_out,
        input_grad,
        mine[0],
        mine[1],
        first_grads[0],
        mine[2],
        first_grads[1],
        first_grads[2],
        mine[3],
        output_weight_grad,
        mine[4],
        mine[5],
        mine[6],
        up_weight_grad,
        up_mine,
        down_weight_grad,
        mine[7],
    )


def solution(mesh):
    rows, vector, matrix = P(("wide", "narrow"), None), P("narrow"), P("narrow", None)
    in_specs = (rows, P(("wide", "narrow")), rows) + tuple(
        matrix if i in (2, 4, 5, 7, 11, 13) else vector for i in range(15)
    )
    out_specs = (rows, rows) + in_specs[3:]
    return jax.shard_map(
        functools.partial(layer, Links(mesh)),
        mesh=mesh,
        in_specs=in_specs,
        out_specs=out_specs,
        check_vma=False,
    )
```

time: 716 us -> 380 us (0.53)
  waiting for transfers between devices: 312 us -> 98.1 us
  matrix products: 204 us -> 0 us
  Pallas kernels: 0 us -> 179 us
  other arithmetic: 54.7 us -> 0.04 us
  blocking collectives: 54.2 us -> 0 us
  starting transfers between devices: 0.51 us -> 43.1 us
  local copies, waits for them, and re-layouts: 64.3 us -> 43.3 us
    dot_general x32 -> x0, matrix products: 204 us -> none  [the longest x6 63.3 us: product(): return jnp.dot(left, right, preferred_element_type=jnp.float32)]
    pallas_call x0 -> x30, Pallas kernels: none -> 179 us  [the longest x11 163 us: run(): pl.pallas_call(inner, out_shape=outs, grid_spec=pltpu.PrefetchScalarGridS...]
    reduce_scatter x6 -> x0, waiting for transfers between devices: 123 us -> none  [the longest x1 60.1 us: shards(): lax.psum_scatter(up_weight_grad.astype(jnp.bfloat16), 'narrow', scatter_d...]
    all_gather x6 -> x0, waiting for transfers between devices: 108 us -> none  [the longest x1 48.4 us: shards(): lax.all_gather(up_weight, 'narrow', axis=0, tiled=True)]
    ppermute x0 -> x45, waiting for transfers between devices: none -> 92.1 us  [move(): return lax.ppermute(value, ('wide', 'narrow'), pairs)]
    psum x1, waiting for transfers between devices: 76.8 us -> 5.95 us  [sum_levels(): return lax.psum(own, 'wide', axis_index_groups=groups)]
    ppermute x0 -> x45, starting transfers between devices: none -> 43 us  [move(): return lax.ppermute(value, ('wide', 'narrow'), pairs)]
    convert_element_type x28 -> x0, other arithmetic: 35.7 us -> none  [the longest x2 14 us: attention_backward(): grad_scores = (probs * (grad_probs - inner)).astype(jnp.bfloat16)]
  transfers between devices with their start and end apart: 13 -> 46, of which waited for: 8 -> 13; matrix products, arithmetic and copies ran while one was open for 37% -> 3% of each run, Pallas kernels for 0% -> 43%
where the time goes in v1:
time: 380 us; the launch traced here: 378 us
  Pallas kernels  179 us (47%)
  waiting for transfers between devices  98.1 us (26%)
  local copies, waits for them, and re-layouts  43.3 us (11%)
  starting transfers between devices  43.1 us (11%)
  between operations  14.8 us (4%)
    pallas_call x11, Pallas kernels, run(): pl.pallas_call(inner, out_shape=outs, grid_spec=pltpu.PrefetchScalarGridS...  163 us
    ppermute x45, waiting for transfers between devices, move(): return lax.ppermute(value, ('wide', 'narrow'), pairs)  92.1 us
    ppermute x45, starting transfers between devices, move(): return lax.ppermute(value, ('wide', 'narrow'), pairs)  43 us
    unnamed x126, local copies, waits for them, and re-layouts  33.3 us
    pallas_call x19, Pallas kernels, small(): pl.pallas_call(inner, out_shape=outs, in_specs=[smem] * len(lead) + [vmem...  15.3 us
  transfers between devices with their start and end apart: 46, of which 13 were waited for; matrix products, arithmetic and copies ran while one was open for 3% of the time, Pallas kernels for 43%

profile of v1, /device:TPU:0, one launch (start us, length us, event | category | flops | bytes accessed | tf_op | source)
XLA Modules:
  0.0 378.0 jit_solution(357937360845429591)
XLA Ops:
  17.7 8.3 %collective-permute-done.2.refs_4_ = bf16[12,192]{1,0:T(8,128)(2,1)S(1)} collective-permute-done((bf16[12,192]{1,0:T(8,128)(2,1)S(1)}, bf16[12,192]{1,0:T(8,128)(2,1)S(1)}, u32[]{:S(2)}, u32[]{:S(2)}) %collective-permute-start.2) | collective-permute-done | bytes 4640 | tf_op jit(solution)/shard_map/ppermute | solution.py:762
  31.6 7.7 %collective-permute-done.4.refs_5_.refs_11_ = bf16[96,2304]{1,0:T(8,128)(2,1)S(1)} collective-permute-done((bf16[96,2304]{1,0:T(8,128)(2,1)S(1)}, bf16[96,2304]{1,0:T(8,128)(2,1)S(1)}, u32[]{:S(2)}, u32[]{:S(2)}) %collective-permute-start.4) | collective-permute-done | bytes 442400 | tf_op jit(solution)/shard_map/ppermute | solution.py:762
  42.2 14.6 %attend.2 = (bf16[768,1024]{1,0:T(8,128)(2,1)}, bf16[1024,768]{1,0:T(8,128)(2,1)}, bf16[1024,768]{1,0:T(8,128)(2,1)}, bf16[1024,768]{1,0:T(8,128)(2,1)}, bf16[10...) custom-call(s32[19]{0:T(128)S(1)} %dynamic-slice_bitcast_fusion.refs_0_.m, ...), custom_call_target="tpu_custom_call" | custom-call | flops 7549747200 | bytes 27357184 | tf_op jit(solution)/shard_map/attend/pallas_call | solution.py:68
  60.7 14.9 %attend.3 = (bf16[768,1024]{1,0:T(8,128)(2,1)}, bf16[1024,768]{1,0:T(8,128)(2,1)}, bf16[1024,768]{1,0:T(8,128)(2,1)}, bf16[1024,768]{1,0:T(8,128)(2,1)}, bf16[10...) custom-call(s32[19]{0:T(128)S(1)} %dynamic-slice_bitcast_fusion.refs, ...), custom_call_target="tpu_custom_call", output_to_operand_aliasing={{0}: (9, {}), {1}: (10, {}), {2}: (11, {}), {3}: (12, {}), ... | custom-call | flops 7549747200 | bytes 49573888 | tf_op jit(solution)/shard_map/attend/pallas_call | solution.py:68
  80.0 20.3 %collective-permute-done.11.refs_5_.refs_4_ = bf16[768,768]{1,0:T(8,128)(2,1)S(1)} collective-permute-done((bf16[768,768]{1,0:T(8,128)(2,1)S(1)}, bf16[768,768]{1,0:T(8,128)(2,1)S(1)}, u32[]{:S(2)}, u32[]{:S(2)}) %collective-permute-start.11) | collective-permute-done | bytes 1179680 | tf_op jit(solution)/shard_map/ppermute | solution.py:762
  101.7 24.3 %feed.1 = (f32[1024,768]{1,0:T(8,128)}, bf16[768,1024]{1,0:T(8,128)(2,1)}, bf16[1024,3072]{1,0:T(8,128)(2,1)}, bf16[1024,3072]{1,0:T(8,128)(2,1)}, bf16[1024,768]{1,0:T(8,128)(2,1)}, /*index=5*/f32[8,768]{1,0:T(8,128)}) custom-call(s32[19]{0:T(128)S(1)} %dynamic-slice_bitcast_fusion.refs_0_.meta, bf16[1024,768]{1,0:T(8,128)(2,1)} %get-tuple-element.107.refs_0_, ...), custom_call_target="tpu_custom_call" | custom-call | flops 27179089920 | bytes 29556736 | tf_op jit(solution)/shard_map/feed/pallas_call | solution.py:68
  128.0 12.3 %down_grad.1 = (bf16[1536,768]{1,0:T(8,128)(2,1)}, bf16[384,768]{1,0:T(8,128)(2,1)}, bf16[384,768]{1,0:T(8,128)(2,1)}, bf16[768,768]{1,0:T(8,128)(2,1)}) custom-call(s32[19]{0:T(128)S(1)} %dynamic-slice_bitcast_fusion.refs_0_.meta, bf16[1024,3072]{1,0:T(8,128)(2,1)} %get-tuple-element.111.refs_0_, bf16[1024,768]{1,0:T(8,128)(2,1)} %get-tuple-element.119.refs_1_.refs_2_, ...), custom_call_target="tpu_custom_call" | custom-call | flops 7247757312 | bytes 12582912 | tf_op jit(solution)/shard_map/down_grad/pallas_call | solution.py:68
  140.8 4.8 %collective-permute-done.14.refs_8_.refs_7_ = bf16[384,768]{1,0:T(8,128)(2,1)S(1)} collective-permute-done((bf16[384,768]{1,0:T(8,128)(2,1)S(1)}, bf16[384,768]{1,0:T(8,128)(2,1)S(1)}, u32[]{:S(2)}, u32[]{:S(2)}) %collective-permute-start.14) | collective-permute-done | bytes 589856 | tf_op jit(solution)/shard_map/ppermute | solution.py:762
  148.5 23.6 %back.1 = (bf16[1024,3072]{1,0:T(8,128)(2,1)}, f32[1024,768]{1,0:T(8,128)}, bf16[1024,768]{1,0:T(8,128)(2,1)}, bf16[1024,768]{1,0:T(8,128)(2,1)}, f32[8,768]{1,0:T(8,128)}, /*index=5*/f32[8,3072]{1,0:T(8,128)}) custom-call(s32[19]{0:T(128)S(1)} %dynamic-slice_bitcast_fusion.refs_0_.meta, bf16[1024,3072]{1,0:T(8,128)(2,1)} %get-tuple-element.118.refs_0_, ...), custom_call_target="tpu_custom_call" | custom-call | flops 16307453952 | bytes 34357248 | tf_op jit(solution)/shard_map/back/pallas_call | solution.py:68
  175.2 9.9 %second_send.1.refs_8_ = bf16[384,3840]{1,0:T(8,128)(2,1)} custom-call(s32[19]{0:T(128)S(1)} %dynamic-slice_bitcast_fusion.refs_0_.meta, bf16[768,1024]{1,0:T(8,128)(2,1)} %get-tuple-element.128.refs_0_, bf16[768,1024]{1,0:T(8,128)(2,1)} %get-tuple-element.117.refs_1_.refs_3_, bf16[1024,3072]{1,0:T(8,128)(2,1)} %get-tuple-element.126.refs_2_, ...), custom_call_target="tpu_custom_call" | custom-call | flops 4529848320 | bytes 13959168 | tf_op jit(solution)/shard_map/second_send/pallas_call | solution.py:68
  187.7 18.8 %attend_back.2 = (bf16[1024,512]{1,0:T(8,128)(2,1)}, bf16[1024,512]{1,0:T(8,128)(2,1)}, bf16[1024,512]{1,0:T(8,128)(2,1)}, bf16[384,1536]{1,0:T(8,128)(2,1)}, bf...) custom-call(s32[19]{0:T(128)S(1)} %dynamic-slice_bitcast_fusion.refs_0_.meta, ...), custom_call_target="tpu_custom_call" | custom-call | flops 10871635968 | bytes 27770880 | tf_op jit(solution)/shard_map/attend_back/pallas_call | solution.py:68
  210.1 10.4 %second_keep.1 = (bf16[96,3840]{1,0:T(8,128)(2,1)}, bf16[96,3840]{1,0:T(8,128)(2,1)}, bf16[192,3840]{1,0:T(8,128)(2,1)}) custom-call(s32[19]{0:T(128)S(1)} %dynamic-slice_bitcast_fusion.refs_0_.meta, bf16[768,1024]{1,0:T(8,128)(2,1)} %get-tuple-element.128.refs_0_, bf16[768,1024]{1,0:T(8,128)(2,1)} %get-tuple-element.117.refs_1_.refs_3_, ...), custom_call_target="tpu_custom_call" | custom-call | flops 4529848320 | bytes 16908288 | tf_op jit(solution)/shard_map/second_keep/pallas_call | solution.py:68
  222.6 15.8 %collective-permute-done.17.refs_1_ = bf16[384,768]{1,0:T(8,128)(2,1)S(1)} collective-permute-done((bf16[384,768]{1,0:T(8,128)(2,1)S(1)}, bf16[384,768]{1,0:T(8,128)(2,1)S(1)}, u32[]{:S(2)}, u32[]{:S(2)}) %collective-permute-start.17) | collective-permute-done | bytes 589856 | tf_op jit(solution)/shard_map/ppermute | solution.py:762
  240.5 3.6 collective-permute-start.23
  244.2 11.4 %attend_back.3 = (bf16[1024,256]{1,0:T(8,128)(2,1)}, bf16[1024,256]{1,0:T(8,128)(2,1)}, bf16[1024,256]{1,0:T(8,128)(2,1)}, bf16[384,768]{1,0:T(8,128)(2,1)}, bf1...) custom-call(s32[19]{0:T(128)S(1)} %dynamic-slice_bitcast_fusion.refs_0_.meta, ...), custom_call_target="tpu_custom_call" | custom-call | flops 5435817984 | bytes 24993792 | tf_op jit(solution)/shard_map/attend_back/pallas_call | solution.py:68
  273.3 11.6 %grad_first.1 = (bf16[1024,768]{1,0:T(8,128)(2,1)}, f32[8,768]{1,0:T(8,128)}) custom-call(s32[19]{0:T(128)S(1)} %dynamic-slice_bitcast_fusion.refs_0_.meta, bf16[1024,768]{1,0:T(8,128)(2,1)} %refs_0_.9, f32[1024,768]{1,0:T(8,128)} %get-tuple-element.153.refs_1_, f32[8,768]{1,0:T(8,128)} %copy-done.34, bf16[1024,512]{1,0:T(8,128)(2,1)} %get-tuple-element.130.refs_4_.refs_3_, ...), custom_call_target="tpu_custom_call" | custom-call | flops 5435817984 | bytes 14598144 | tf_op jit(solution)/shard_map/grad_first/pallas_call | solution.py:68
  288.1 3.7 collective-permute-start.36
  293.1 11.5 %down_out.1.refs_4_ = bf16[1024,768]{1,0:T(8,128)(2,1)} custom-call(s32[19]{0:T(128)S(1)} %dynamic-slice_bitcast_fusion.refs_0_.meta, bf16[1024,3072]{1,0:T(8,128)(2,1)} %get-tuple-element.111.refs_0_, f32[1024,768]{1,0:T(8,128)} %get-tuple-element.112.refs_2_.refs_1_, f32[8,768]{1,0:T(8,128)} %copy-done.34, bf16[768,768]{1,0:T(8,128)(2,1)} %refs_3_.1, ...), custom_call_target="tpu_custom_call" | custom-call | flops 7247757312 | bytes 15753216 | tf_op jit(solution)/shard_map/down_out/pallas_call | solution.py:68
  304.6 6.5 %collective-permute-done.36.refs_3_ = bf16[96,1536]{1,0:T(8,128)(2,1)S(1)} collective-permute-done((bf16[96,1536]{1,0:T(8,128)(2,1)S(1)}, bf16[96,1536]{1,0:T(8,128)(2,1)S(1)}, u32[]{:S(2)}, u32[]{:S(2)}) %collective-permute-start.36) | collective-permute-done | bytes 294944 | tf_op jit(solution)/shard_map/ppermute | solution.py:762
  312.8 21.0 %collective-permute-done.39.refs_2_ = bf16[384,768]{1,0:T(8,128)(2,1)S(1)} collective-permute-done((bf16[384,768]{1,0:T(8,128)(2,1)S(1)}, bf16[384,768]{1,0:T(8,128)(2,1)S(1)}, u32[]{:S(2)}, u32[]{:S(2)}) %collective-permute-start.39) | collective-permute-done | bytes 589856 | tf_op jit(solution)/shard_map/ppermute | solution.py:762
  335.2 5.9 %all-reduce.2.cloned.1.call-done.refs_1_ = bf16[96,3840]{1,0:T(8,128)(2,1)} async-done(((bf16[96,3840]{1,0:T(8,128)(2,1)}), bf16[96,3840]{1,0:T(8,128)(2,1)}) %all-reduce.2.cloned.1.call-update) | async-done | bytes 737296 | tf_op jit(solution)/shard_map/psum | solution.py:820
  343.5 3.7 collective-permute-start.31
  349.4 3.2 collective-permute-start.41
  359.2 3.0 collective-permute-done.41.refs_1_
  (246 shorter events, 92.2 us)
Async XLA Ops:
  7.2 334.0 %all-reduce.2.cloned.1.call-start = ((), (), s32[]{:S(2)}) async-start(), calls=%async_computation | async-start | bytes 1474560 | tf_op jit(solution)/shard_map/psum | solution.py:820
  10.3 17.0 %collective-permute-start.3 = (bf16[192,2304]{1,0:T(8,128)(2,1)S(1)}, bf16[192,2304]{1,0:T(8,128)(2,1)S(1)}, u32[]{:S(2)}, u32[]{:S(2)}) collective-permute-start(bf16[192,2304]{1,0:T(8,128)(2,1)S(1)} %pack.2.refs_5_.refs_3_.refs_9_), channel_id=1, source_target_pairs={{0,1},{1,0},{2,3},{3,2},{4,6},{5,7},{6,4},{7,5},{8,9},{9,8},{10,11... | collective-permute-start | bytes 2654216 | tf_op jit(solution)/shard_map/ppermute | solution.py:762
  30.0 26.7 %collective-permute-start.7 = (bf16[192,3840]{1,0:T(8,128)(2,1)S(1)}, bf16[192,3840]{1,0:T(8,128)(2,1)S(1)}, u32[]{:S(2)}, u32[]{:S(2)}) collective-permute-start(bf16[192,3840]{1,0:T(8,128)(2,1)S(1)} %pack.3.refs_8_.refs_6_.refs_9_), channel_id=1, source_target_pairs={{0,1},{1,0},{2,3},{3,2},{4,6},{5,7},{6,4},{7,5},{8,9},{9,8},{10,11... | collective-permute-start | bytes 4423688 | tf_op jit(solution)/shard_map/ppermute | solution.py:762
  59.3 19.0 %collective-permute-start.8 = (bf16[96,3840]{1,0:T(8,128)(2,1)S(1)}, bf16[96,3840]{1,0:T(8,128)(2,1)S(1)}, u32[]{:S(2)}, u32[]{:S(2)}) collective-permute-start(bf16[96,3840]{1,0:T(8,128)(2,1)S(1)} %copies.4.refs_16_), channel_id=1, source_target_pairs={{0,2},{1,3},{2,0},{3,1},{4,5},{5,4},{6,7},{7,6},{8,10},{9,11},{10,... | collective-permute-start | bytes 2211848 | tf_op jit(solution)/shard_map/ppermute | solution.py:762
  59.4 40.9 %collective-permute-start.9 = (bf16[192,3840]{1,0:T(8,128)(2,1)S(1)}, bf16[192,3840]{1,0:T(8,128)(2,1)S(1)}, u32[]{:S(2)}, u32[]{:S(2)}) collective-permute-start(bf16[192,3840]{1,0:T(8,128)(2,1)S(1)} %collective-permute-done.7.refs_1_.refs_7_.refs_10_), channel_id=1, source_target_pairs={{0,4},{1,5},{2,6},{3,7},{4,0},{5,1},{6,2},{7,3},{8,12},{9,13},{10,... | collective-permute-start | bytes 4423688 | tf_op jit(solution)/shard_map/ppermute | solution.py:762
  77.7 22.6 %collective-permute-start.11 = (bf16[768,768]{1,0:T(8,128)(2,1)S(1)}, bf16[768,768]{1,0:T(8,128)(2,1)S(1)}, u32[]{:S(2)}, u32[]{:S(2)}) collective-permute-start(bf16[768,768]{1,0:T(8,128)(2,1)S(1)} %get-tuple-element.113), channel_id=1, source_target_pairs={{0,1},{1,0},{2,3},{3,2},{4,6},{5,7},{6,4},{7,5},{8,9},{9,8},{10,11... | collective-permute-start | bytes 3538952 | tf_op jit(solution)/shard_map/ppermute | solution.py:762
  78.3 22.0 %collective-permute-start.10 = (bf16[96,3840]{1,0:T(8,128)(2,1)S(1)}, bf16[96,3840]{1,0:T(8,128)(2,1)S(1)}, u32[]{:S(2)}, u32[]{:S(2)}) collective-permute-start(bf16[96,3840]{1,0:T(8,128)(2,1)S(1)} %collective-permute-done.8.refs_8_.refs_11_), channel_id=1, source_target_pairs={{0,4},{1,5},{2,6},{3,7},{4,0},{5,1},{6,2},{7,3},{8,12},{9,13},{10,... | collective-permute-start | bytes 2211848 | tf_op jit(solution)/shard_map/ppermute | solution.py:762
  78.7 62.0 %collective-permute-start.12 = (bf16[384,768]{1,0:T(8,128)(2,1)S(1)}, bf16[384,768]{1,0:T(8,128)(2,1)S(1)}, u32[]{:S(2)}, u32[]{:S(2)}) collective-permute-start(bf16[384,768]{1,0:T(8,128)(2,1)S(1)} %get-tuple-element.110.refs_11_), channel_id=1, source_target_pairs={{0,3},{1,2},{2,1},{3,0},{4,7},{5,6},{6,5},{7,4},{8,11},{9,10},{10,... | collective-permute-start | bytes 1769480 | tf_op jit(solution)/shard_map/ppermute | solution.py:762
  100.3 45.3 %collective-permute-start.13 = (bf16[768,768]{1,0:T(8,128)(2,1)S(1)}, bf16[768,768]{1,0:T(8,128)(2,1)S(1)}, u32[]{:S(2)}, u32[]{:S(2)}) collective-permute-start(bf16[768,768]{1,0:T(8,128)(2,1)S(1)} %collective-permute-done.11.refs_5_.refs_4_), channel_id=1, source_target_pairs={{0,4},{1,5},{2,6},{3,7},{4,0},{5,1},{6,2},{7,3},{8,12},{9,13},{10,... | collective-permute-start | bytes 3538952 | tf_op jit(solution)/shard_map/ppermute | solution.py:762
  140.3 31.9 %collective-permute-start.15 = (bf16[1536,768]{1,0:T(8,128)(2,1)}, bf16[1536,768]{1,0:T(8,128)(2,1)S(1)}, u32[]{:S(2)}, u32[]{:S(2)}) collective-permute-start(bf16[1536,768]{1,0:T(8,128)(2,1)} %get-tuple-element.120.refs_14_), channel_id=1, source_target_pairs={{0,4},{1,5},{2,6},{3,7},{4,0},{5,1},{6,2},{7,3},{8,12},{9,13},{10,... | collective-permute-start | bytes 7077896 | tf_op jit(solution)/shard_map/ppermute | solution.py:762
  185.1 23.3 %collective-permute-start.19 = (bf16[384,3840]{1,0:T(8,128)(2,1)}, bf16[384,3840]{1,0:T(8,128)(2,1)S(1)}, u32[]{:S(2)}, u32[]{:S(2)}) collective-permute-start(bf16[384,3840]{1,0:T(8,128)(2,1)} %second_send.1.refs_8_), channel_id=1, source_target_pairs={{0,4},{1,5},{2,6},{3,7},{4,0},{5,1},{6,2},{7,3},{8,12},{9,13},{10,... | collective-permute-start | bytes 8847368 | tf_op jit(solution)/shard_map/ppermute | solution.py:762
  185.3 21.5 %collective-permute-start.16 = (bf16[768,768]{1,0:T(8,128)(2,1)S(1)}, bf16[768,768]{1,0:T(8,128)(2,1)S(1)}, u32[]{:S(2)}, u32[]{:S(2)}) collective-permute-start(bf16[768,768]{1,0:T(8,128)(2,1)S(1)} %sums_of.9.refs_4_), channel_id=1, source_target_pairs={{0,1},{1,0},{2,3},{3,2},{4,6},{5,7},{6,4},{7,5},{8,9},{9,8},{10,11... | collective-permute-start | bytes 3538952 | tf_op jit(solution)/shard_map/ppermute | solution.py:762
  206.4 16.2 %collective-permute-start.18 = (bf16[384,1536]{1,0:T(8,128)(2,1)}, bf16[384,1536]{1,0:T(8,128)(2,1)S(1)}, u32[]{:S(2)}, u32[]{:S(2)}) collective-permute-start(bf16[384,1536]{1,0:T(8,128)(2,1)} %get-tuple-element.134), channel_id=1, source_target_pairs={{0,4},{1,5},{2,6},{3,7},{4,0},{5,1},{6,2},{7,3},{8,12},{9,13},{10,... | collective-permute-start | bytes 3538952 | tf_op jit(solution)/shard_map/ppermute | solution.py:762
  220.6 36.9 %collective-permute-start.22 = (bf16[192,3840]{1,0:T(8,128)(2,1)}, bf16[192,3840]{1,0:T(8,128)(2,1)S(1)}, u32[]{:S(2)}, u32[]{:S(2)}) collective-permute-start(bf16[192,3840]{1,0:T(8,128)(2,1)} %get-tuple-element.144), channel_id=1, source_target_pairs={{0,1},{1,0},{2,3},{3,2},{4,6},{5,7},{6,4},{7,5},{8,9},{9,8},{10,11... | collective-permute-start | bytes 4423688 | tf_op jit(solution)/shard_map/ppermute | solution.py:762
  222.1 16.3 %collective-permute-start.17 = (bf16[384,768]{1,0:T(8,128)(2,1)S(1)}, bf16[384,768]{1,0:T(8,128)(2,1)S(1)}, u32[]{:S(2)}, u32[]{:S(2)}) collective-permute-start(bf16[384,768]{1,0:T(8,128)(2,1)S(1)} %get-tuple-element.132.refs_5_), channel_id=1, source_target_pairs={{0,2},{1,3},{2,0},{3,1},{4,5},{5,4},{6,7},{7,6},{8,10},{9,11},{10,... | collective-permute-start | bytes 1769480 | tf_op jit(solution)/shard_map/ppermute | solution.py:762
  240.5 17.0 %collective-permute-start.23 = (bf16[384,768]{1,0:T(8,128)(2,1)S(1)}, bf16[384,768]{1,0:T(8,128)(2,1)S(1)}, u32[]{:S(2)}, u32[]{:S(2)}) collective-permute-start(bf16[384,768]{1,0:T(8,128)(2,1)S(1)} %get-tuple-element.136.refs_8_.refs_3_), channel_id=1, source_target_pairs={{0,8},{1,9},{2,10},{3,11},{4,12},{5,13},{6,14},{7,15},{24,16},{25,... | collective-permute-start | bytes 1769480 | tf_op jit(solution)/shard_map/ppermute | solution.py:762
  260.6 24.3 %collective-permute-start.26 = (bf16[96,3840]{1,0:T(8,128)(2,1)}, bf16[96,3840]{1,0:T(8,128)(2,1)S(1)}, u32[]{:S(2)}, u32[]{:S(2)}) collective-permute-start(bf16[96,3840]{1,0:T(8,128)(2,1)} %get-tuple-element.146.refs_6_), channel_id=1, source_target_pairs={{0,2},{1,3},{2,0},{3,1},{4,5},{5,4},{6,7},{7,6},{8,10},{9,11},{10,... | collective-permute-start | bytes 2211848 | tf_op jit(solution)/shard_map/ppermute | solution.py:762
  266.3 18.7 %collective-permute-start.27 = (bf16[384,768]{1,0:T(8,128)(2,1)}, bf16[384,768]{1,0:T(8,128)(2,1)S(1)}, u32[]{:S(2)}, u32[]{:S(2)}) collective-permute-start(bf16[384,768]{1,0:T(8,128)(2,1)} %copy-done.18), channel_id=1, source_target_pairs={{8,16},{9,17},{10,18},{11,19},{12,20},{13,21},{14,22},{15,23},{16,... | collective-permute-start | bytes 1769480 | tf_op jit(solution)/shard_map/ppermute | solution.py:762
  287.7 16.9 %collective-permute-start.35 = (bf16[96,768]{1,0:T(8,128)(2,1)S(1)}, bf16[96,768]{1,0:T(8,128)(2,1)S(1)}, u32[]{:S(2)}, u32[]{:S(2)}) collective-permute-start(bf16[96,768]{1,0:T(8,128)(2,1)S(1)} %get-tuple-element.159.refs_8_), channel_id=1, source_target_pairs={{0,2},{1,3},{2,0},{3,1},{4,5},{5,4},{6,7},{7,6},{8,10},{9,11},{10,... | collective-permute-start | bytes 442376 | tf_op jit(solution)/shard_map/ppermute | solution.py:762
  288.1 23.1 %collective-permute-start.36 = (bf16[96,1536]{1,0:T(8,128)(2,1)S(1)}, bf16[96,1536]{1,0:T(8,128)(2,1)S(1)}, u32[]{:S(2)}, u32[]{:S(2)}) collective-permute-start(bf16[96,1536]{1,0:T(8,128)(2,1)S(1)} %get-tuple-element.167.refs_2_), channel_id=1, source_target_pairs={{0,8},{1,9},{2,10},{3,11},{4,12},{5,13},{6,14},{7,15},{8,0},{9,1},... | collective-permute-start | bytes 884744 | tf_op jit(solution)/shard_map/ppermute | solution.py:762
  291.8 42.0 %collective-permute-start.39 = (bf16[384,768]{1,0:T(8,128)(2,1)S(1)}, bf16[384,768]{1,0:T(8,128)(2,1)S(1)}, u32[]{:S(2)}, u32[]{:S(2)}) collective-permute-start(bf16[384,768]{1,0:T(8,128)(2,1)S(1)} %get-tuple-element.170.refs_1_), channel_id=1, source_target_pairs={{8,0},{9,1},{10,2},{11,3},{12,4},{13,5},{14,6},{15,7},{16,24},{17,... | collective-permute-start | bytes 1769480 | tf_op jit(solution)/shard_map/ppermute | solution.py:762
  312.7 34.5 %collective-permute-start.38 = (bf16[96,1536]{1,0:T(8,128)(2,1)S(1)}, bf16[96,1536]{1,0:T(8,128)(2,1)S(1)}, u32[]{:S(2)}, u32[]{:S(2)}) collective-permute-start(bf16[96,1536]{1,0:T(8,128)(2,1)S(1)} %get-tuple-element.169.refs_2_), channel_id=1, source_target_pairs={{0,16},{1,17},{2,18},{3,19},{4,20},{5,21},{6,22},{7,23},{8,24},{9,... | collective-permute-start | bytes 884744 | tf_op jit(solution)/shard_map/ppermute | solution.py:762
  334.4 20.8 %collective-permute-start.42 = (bf16[384,768]{1,0:T(8,128)(2,1)S(1)}, bf16[384,768]{1,0:T(8,128)(2,1)S(1)}, u32[]{:S(2)}, u32[]{:S(2)}) collective-permute-start(bf16[384,768]{1,0:T(8,128)(2,1)S(1)} %pick.1.refs_4_.refs_1_), channel_id=1, source_target_pairs={{0,4},{1,5},{2,6},{3,7},{4,0},{5,1},{6,2},{7,3},{8,12},{9,13},{10,... | collective-permute-start | bytes 1769480 | tf_op jit(solution)/shard_map/ppermute | solution.py:762
  341.2 26.6 %collective-permute-start.44 = (bf16[96,3840]{1,0:T(8,128)(2,1)}, bf16[96,3840]{1,0:T(8,128)(2,1)S(1)}, u32[]{:S(2)}, u32[]{:S(2)}) collective-permute-start(bf16[96,3840]{1,0:T(8,128)(2,1)} %all-reduce.2.cloned.1.call-done.refs_1_), channel_id=1, source_target_pairs={{0,4},{1,5},{2,6},{3,7},{4,0},{5,1},{6,2},{7,3},{8,12},{9,13},{10,... | collective-permute-start | bytes 2211848 | tf_op jit(solution)/shard_map/ppermute | solution.py:762
  (85 other events, 692.3 us)
Sparse Core Ops, SparseCore 0:
  287.8 53.3 all-reduce.1

commit v2 on v1

--- a/solution.py
+++ b/solution.py
@@ -51,10 +51,22 @@
 
 class Order:
     def __init__(self, meta):
-        self.meta, self.last = meta, []
+        self.meta, self.last, self.far = meta, [], []
 
     def run(
-        self, name, body, ins, in_specs, outs, out_specs, grid, scratch, macs, limit, alias={}
+        self,
+        name,
+        body,
+        ins,
+        in_specs,
+        outs,
+        out_specs,
+        grid,
+        scratch,
+        macs,
+        limit,
+        alias={},
+        near=False,
     ):
         moved = sum(a.size * a.dtype.itemsize for a in ins)
         moved += sum(o.size * o.dtype.itemsize for o in outs)
@@ -63,8 +75,12 @@
         def inner(meta, *refs):
             body(meta, *refs[:used], *refs[used + extra :])
 
-        ins = [pltpu.with_memory_space_constraint(a, pltpu.HBM) for a in ins]
-        outs = [pltpu.HBM(o.shape, o.dtype) for o in outs]
+        ins = [
+            a if spec is ANY else pltpu.with_memory_space_constraint(a, pltpu.HBM)
+            for a, spec in zip(ins, in_specs)
+        ]
+        if not near:
+            outs = [pltpu.HBM(o.shape, o.dtype) for o in outs]
         got = pl.pallas_call(
             inner,
             out_shape=outs,
@@ -77,49 +93,80 @@
             ),
             input_output_aliases=alias,
             compiler_params=pltpu.CompilerParams(vmem_limit_bytes=limit * 2**20),
-            cost_estimate=pl.CostEstimate(
-                flops=int(2 * macs * 1.5), bytes_accessed=moved, transcendentals=0
-            ),
+            cost_estimate=pl.CostEstimate(flops=1, bytes_accessed=1 if near else 4 * 10**8, transcendentals=0),
             name=name,
-        )(self.meta, *ins, *self.last)
+        )(self.meta, *ins, *self.tokens())
         self.last = [got[0]]
+        if not near:
+            self.far += got
         return got
 
-    def small(self, name, body, ins, outs, meta=False):
-        moved = sum(a.size * a.dtype.itemsize for a in [*ins, *outs])
+    def tokens(self):
+        return [
+            pltpu.with_memory_space_constraint(t, pltpu.HBM)
+            if any(t is a for a in self.far)
+            else t
+            for t in self.last
+        ]
+
+    def small(self, name, body, ins, outs, scratch=()):
         used, extra = len(ins), len(self.last)
-        lead = [self.meta] if meta else []
-
-        def inner(*refs):
-            held, refs = refs[: len(lead)], refs[len(lead) :]
-            body(*held, *refs[:used], *refs[used + extra :])
+        far = [any(a is b for b in self.far) for a in ins]
+        held = [i for i in range(used) if far[i]]
+        wait = len(held)
+
+        def inner(meta, *refs):
+            inputs, refs = list(refs[:used]), refs[used + extra :]
+            outputs, refs = refs[: len(outs)], refs[len(outs) :]
+            buffers, rest = refs[:wait], refs[wait:]
+            moves = []
+            for n, i in enumerate(held):
+                moves.append(pltpu.make_async_copy(inputs[i], buffers[n], rest[0].at[n]))
+                inputs[i] = buffers[n]
+            for move in moves:
+                move.start()
+            for move in moves:
+                move.wait()
+            body(meta, *inputs, *outputs, *rest[1 if wait else 0 :])
 
         vmem = pl.BlockSpec(memory_space=pltpu.VMEM)
-        smem = pl.BlockSpec(memory_space=pltpu.SMEM)
         got = pl.pallas_call(
             inner,
             out_shape=outs,
-            in_specs=[smem] * len(lead) + [vmem] * used + [ANY] * extra,
+            in_specs=[pl.BlockSpec(memory_space=pltpu.SMEM)]
+            + [ANY if f else vmem for f in far]
+            + [ANY] * extra,
             out_specs=[vmem] * len(outs),
-            compiler_params=pltpu.CompilerParams(vmem_limit_bytes=16 * 2**20),
-            cost_estimate=pl.CostEstimate(flops=0, bytes_accessed=moved, transcendentals=0),
+            scratch_shapes=[pltpu.VMEM(ins[i].shape, ins[i].dtype) for i in held]
+            + ([pltpu.SemaphoreType.DMA((wait,))] if wait else [])
+            + list(scratch),
+            compiler_params=pltpu.CompilerParams(vmem_limit_bytes=20 * 2**20),
+            cost_estimate=pl.CostEstimate(flops=1, bytes_accessed=1, transcendentals=0),
             name=name,
-        )(*lead, *ins, *self.last)
+        )(
+            self.meta,
+            *[
+                pltpu.with_memory_space_constraint(a, pltpu.HBM) if f else a
+                for a, f in zip(ins, far)
+            ],
+            *self.tokens(),
+        )
         self.last = [got[0]]
         return got
 
 
-def fill(meta, pieces, target, sems):
+def fill(meta, pieces, target, sems, cols=None):
     count = 1 if len(pieces) == 1 else len(pieces)
     half = target.shape[0] // 8
     copies = []
     for i in range(count):
-        start = pl.multiple_of(meta[i] * half, half) if count > 1 else 0
-        copies.append(
-            pltpu.make_async_copy(
-                pieces[i], target.at[pl.ds(start, pieces[i].shape[0])], sems.at[i]
-            )
-        )
+        place = meta[19] if count == 4 and i == 2 else meta[i]
+        start = pl.multiple_of(place * half, half) if count > 1 else 0
+        rows = pl.ds(start, pieces[i].shape[0])
+        src, dst = pieces[i], target.at[rows]
+        if cols is not None:
+            src, dst = src.at[:, cols], target.at[rows, cols]
+        copies.append(pltpu.make_async_copy(src, dst, sems.at[i]))
     return copies
 
 
@@ -143,15 +190,52 @@
 
 
 def pack(order, parts):
+    rows = parts[0].shape[0]
     width = sum(p.shape[1] for p in parts)
-
-    def body(*refs):
-        at = 0
-        for src in refs[:-1]:
-            refs[-1][:, at : at + src.shape[1]] = src[...]
+    count = len(parts)
+
+    def body(meta, *refs):
+        out, sems = refs[count:]
+        moves, at = [], 0
+        for i, src in enumerate(refs[:count]):
+            cols = out.at[:, at : at + src.shape[1]]
+            moves.append(pltpu.make_async_copy(src, cols, sems.at[i]))
             at += src.shape[1]
-
-    return order.small("pack", body, parts, [shape((parts[0].shape[0], width), bf16)])[0]
+        for move in moves:
+            move.start()
+        for move in moves:
+            move.wait()
+
+    return order.run(
+        "pack",
+        body,
+        [pltpu.with_memory_space_constraint(p, pltpu.HBM) for p in parts],
+        [ANY] * count,
+        [shape((rows, width), bf16)],
+        [whole((rows, width))],
+        (1,),
+        [pltpu.SemaphoreType.DMA((count,))],
+        0,
+        16,
+        near=True,
+    )[0]
+
+
+def gate(order, value):
+    return order.run(
+        "gate",
+        lambda meta, *refs: None,
+        [value],
+        [ANY],
+        [shape(value.shape, value.dtype)],
+        [ANY],
+        (1,),
+        [],
+        0,
+        16,
+        alias={1: 0},
+        near=True,
+    )[0]
 
 
 def copies(order, halves, wholes=()):
@@ -166,27 +250,65 @@
             else:
                 dst[...] = src[...]
 
-    return order.small("copies", body, ins, [shape(d, bf16) for d in dims], True)
-
-
-def sums_of(order, plan):
-    ins, where = [], {}
-    for _, terms in plan:
-        for array, _ in terms:
-            if id(array) not in where:
-                where[id(array)] = len(ins)
+    return order.small("copies", body, ins, [shape(d, bf16) for d in dims])
+
+
+def fetch(order, *arrays):
+    count = len(arrays)
+
+    def body(meta, *refs):
+        moves = [
+            pltpu.make_async_copy(refs[i], refs[count + i], refs[-1].at[i]) for i in range(count)
+        ]
+        for move in moves:
+            move.start()
+        for move in moves:
+            move.wait()
+
+    return order.run(
+        "fetch",
+        body,
+        [pltpu.with_memory_space_constraint(a, pltpu.HBM) for a in arrays],
+        [ANY] * count,
+        [shape(a.shape, bf16) for a in arrays],
+        [whole(a.shape) for a in arrays],
+        (1,),
+        [pltpu.SemaphoreType.DMA((count,))],
+        0,
+        20,
+        near=True,
+    )
+
+
+def sums_of(order, *plan):
+    ins = []
+    for parts in plan:
+        for array, _ in sum(parts, []):
+            if not any(array is other for other in ins):
                 ins.append(array)
-
-    def body(*refs):
-        for (rows, terms), out in zip(plan, refs[len(ins) :]):
-            total = None
-            for array, start in terms:
-                term = refs[where[id(array)]][start : start + rows].astype(f32)
-                total = term if total is None else total + term
-            out[...] = total.astype(bf16)
-
-    dims = [(rows, terms[0][0].shape[1]) for rows, terms in plan]
-    return order.small("sums_of", body, ins, [shape(d, bf16) for d in dims])
+    where = lambda array: [i for i, other in enumerate(ins) if other is array][0]
+    places = [[[(where(a), index) for a, index in terms] for terms in parts] for parts in plan]
+
+    def body(meta, *refs):
+        for parts, out in zip(places, refs[len(ins) :]):
+            at = 0
+            for terms in parts:
+                total = None
+                for i, index in terms:
+                    term = refs[i][index].astype(f32)
+                    total = term if total is None else total + term
+                rows = slice(at, at + total.shape[-2])
+                out[..., rows, :] = total.astype(bf16)
+                at += total.shape[-2]
+
+    outs = []
+    for parts in plan:
+        dims = [
+            jax.eval_shape(lambda a, i=terms[0][1]: a[i], terms[0][0]).shape for terms in parts
+        ]
+        rows = sum(d[-2] for d in dims)
+        outs.append(shape((*dims[0][:-2], rows, dims[0][-1]), bf16))
+    return order.small("sums_of", body, ins, outs)
 
 
 def pick(order, own, got):
@@ -194,27 +316,33 @@
         inner = jnp.full(out.shape, meta[14], jnp.int32) == 1
         out[...] = jnp.where(inner, own[...], got[...])
 
-    return order.small("pick", body, [own, got], [shape(own.shape, bf16)], True)[0]
-
-
-def finish(order, pairs, plan):
+    return order.small("pick", body, [own, got], [shape(own.shape, bf16)])[0]
+
+
+def finish(order, half, pairs, plan, last=0):
     flat = [a for pair in pairs for a in pair]
-    half = flat[0].shape[0]
 
     def body(meta, *refs):
         core = meta[13]
         for (width, parts), out in zip(plan, refs[len(flat) :]):
             at = 0
-            for which, first, cols in parts:
+            for which, block, first, cols in parts:
                 for i in range(2):
                     place = core if i == 0 else 1 - core
                     rows = pl.ds(pl.multiple_of(place * half, half), half)
-                    value = refs[2 * which + i][:, first : first + cols]
+                    value = refs[2 * which + i][
+                        block * half : (block + 1) * half, first : first + cols
+                    ]
                     out[rows, at : at + cols] = value.astype(f32)
                 at += cols
+        if last:
+            own, other = [ref[ref.shape[0] - last :].astype(f32) for ref in refs[:2]]
+            refs[-1][...] = own + other
 
     outs = [shape((2 * half, width), f32) for width, _ in plan]
-    return order.small("finish", body, flat, outs, True)
+    if last:
+        outs.append(shape((last, D), f32))
+    return order.small("finish", body, flat, outs)
 
 
 def attend(order, tokens, vec, segs, pieces, at_seq, before):
@@ -326,7 +454,7 @@
         ub[...] = jnp.concatenate([r[8 + i : 9 + i] for r in rows for i in range(4)], 1)
 
     outs = [shape((8, D), f32), shape((1, FF), f32)]
-    return order.small("vectors", body, sources, outs, True)
+    return order.small("vectors", body, sources, outs)
 
 
 def gelu_both(x):
@@ -346,8 +474,19 @@
     rows = tokens.shape[0]
 
     def body(meta, att, tok, og, seg, vec, ub, *rest):
-        pieces, (mid, sn_t, hid, slope, gb, down_sum, w, sems) = rest[:count], rest[count:]
-        first_step(fill(meta, pieces, w, sems))
+        pieces, rest = rest[:count], rest[count:]
+        mid, sn_t, hid, slope, gb, down_sum, w, sems, sems_up = rest
+        first = fill(meta, pieces, w, sems, slice(FF, FF + D))
+        others = fill(meta, pieces, w, sems_up, slice(0, FF))
+        begin = pl.program_id(0) == 0
+
+        @pl.when(begin)
+        def _():
+            for copy in [*first, *others]:
+                copy.start()
+            for copy in first:
+                copy.wait()
+
         m = tok[...].astype(f32) + dot(att[...], w[:, FF:]) + vec[4:5]
         mid[...] = m
         low = (standard(m)[0] * vec[5:6] + vec[6:7]).astype(bf16)
@@ -360,6 +499,12 @@
             down_sum[...] = jnp.zeros_like(down_sum)
 
         down_sum[0:1] += column_sum(grad)
+
+        @pl.when(begin)
+        def _():
+            for copy in others:
+                copy.wait()
+
         for at in range(0, FF, 512):
             pre = dot(low, w[:, at : at + 512]) + ub[:, at : at + 512]
             act, der = gelu_both(pre)
@@ -383,7 +528,7 @@
         ],
         [blk, pl.BlockSpec((D, TILE), lambda at, m: (0, at)), wide, wide, blk, whole((8, D))],
         (rows // TILE,),
-        [pltpu.VMEM((D, FF + D), bf16), pltpu.SemaphoreType.DMA((count,))],
+        [pltpu.VMEM((D, FF + D), bf16)] + [pltpu.SemaphoreType.DMA((count,))] * 2,
         rows * D * (FF + D) * 3,
         32,
     )
@@ -429,21 +574,30 @@
     def body(meta, slope, mid, gb, vec, *rest):
         downs, pieces, rest = rest[:nd], rest[nd : nd + count], rest[nd + count :]
         gpre, gmid, gattn, gatt, sums, up_sum, wd, w, sems_d, sems = rest
-        first_step(fill(meta, downs, wd, sems_d) + fill(meta, pieces, w, sems))
-
-        @pl.when(pl.program_id(0) == 0)
-        def _():
+        first, others = fill(meta, downs, wd, sems_d), fill(meta, pieces, w, sems)
+        begin = pl.program_id(0) == 0
+
+        @pl.when(begin)
+        def _():
+            for copy in [*first, *others]:
+                copy.start()
             sums[...] = jnp.zeros_like(sums)
             up_sum[...] = jnp.zeros_like(up_sum)
-
-        grad = None
+            for copy in first:
+                copy.wait()
+
         for at in range(0, FF, 512):
             cols = slice(at, at + 512)
             low = (dot(gb[...], wd[cols], NT) * slope[:, cols].astype(f32)).astype(bf16)
             gpre[:, cols] = low
             up_sum[0:1, cols] += column_sum(low.astype(f32))
-            term = dot(low, w[:, cols], NT)
-            grad = term if grad is None else grad + term
+
+        @pl.when(begin)
+        def _():
+            for copy in others:
+                copy.wait()
+
+        grad = dot(gpre[...], w[:, :FF], NT)
         hat, rate = standard(mid[...])
         sums[0:1] += column_sum(grad * hat)
         sums[1:2] += column_sum(grad)
@@ -535,17 +689,24 @@
         def _():
             for copy in moves():
                 copy.wait()
+            for i in range(blocks):
+                right = grads[:, i * D : (i + 1) * D]
+                rows_of = slice(i * BAND, (i + 1) * BAND)
+                low = dot(held[...], right).astype(bf16)
+                for j in range(4):
+                    send[j, rows_of] = low[j * BAND : (j + 1) * BAND]
+                own[rows_of] = low[4 * BAND : 5 * BAND]
+                near[rows_of] = low[5 * BAND : 6 * BAND]
+                for j in range(2):
+                    far[j, rows_of] = low[(6 + j) * BAND : (7 + j) * BAND]
             right = grads[...]
-            send[...] = dot(held[: 4 * BAND], right).astype(bf16)
-            kept = dot(held[4 * BAND :], right).astype(bf16)
-            own[...] = kept[:BAND]
-            near[...] = kept[BAND : 2 * BAND]
-            far[...] = kept[2 * BAND :]
             sums[...] = jnp.broadcast_to(column_sum(right.astype(f32)), sums.shape)
 
     blk = pl.BlockSpec((LEN, PAIR), lambda s, p, m: (s, p + first))
     out = pl.BlockSpec((LEN, PAIR), lambda s, p, m: (s, p))
-    widths = [4 * BAND, BAND, BAND, 2 * BAND]
+    blocks = 3 * width // D
+    bands = [(n, blocks * BAND, D) for n in (4, 2)]
+    bands = [bands[0], bands[0][1:], bands[0][1:], bands[1]]
     return order.run(
         "attend_back",
         body,
@@ -559,9 +720,9 @@
             ANY,
         ],
         [shape((rows, width), bf16)] * 3
-        + [shape((n, 3 * width), bf16) for n in widths]
+        + [shape(d, bf16) for d in bands]
         + [shape((8, 3 * width), f32)],
-        [out] * 3 + [whole((n, 3 * width)) for n in widths] + [whole((8, 3 * width))],
+        [out] * 3 + [whole(d) for d in bands] + [whole((8, 3 * width))],
         (count, pairs),
         [
             pltpu.VMEM((rows, 3 * width), bf16),
@@ -625,7 +786,7 @@
 
         @pl.when(at < 4)
         def _():
-            send[...] = low
+            send[0] = low
 
         @pl.when(at == 4)
         def _():
@@ -637,19 +798,19 @@
 
         @pl.when(at >= 6)
         def _():
-            far[...] = low
+            far[0] = low
 
     return order.run(
         "down_grad",
         body,
         [hidden, gb],
         [pl.BlockSpec((rows, band), lambda j, m: (0, m[5 + j])), whole((rows, D))],
-        [shape((n * band, D), bf16) for n in (4, 1, 1, 2)],
+        [shape(d, bf16) for d in ((4, band, D), (band, D), (band, D), (2, band, D))],
         [
-            pl.BlockSpec((band, D), lambda j, m: (jnp.minimum(j, 3), 0)),
+            pl.BlockSpec((1, band, D), lambda j, m: (jnp.minimum(j, 3), 0, 0)),
             whole((band, D)),
             whole((band, D)),
-            pl.BlockSpec((band, D), lambda j, m: (jnp.maximum(j - 6, 0), 0)),
+            pl.BlockSpec((1, band, D), lambda j, m: (jnp.maximum(j - 6, 0), 0, 0)),
         ],
         (8,),
         [],
@@ -658,93 +819,73 @@
     )
 
 
-def weight_grad(name, order, left, first, recv):
-    rows = left[0][0].shape[1]
-    width = min(r.shape[1] for _, rights in left for r in rights)
-    width = min(width, D)
-    plan = []
-    flat = []
-    for i, (_, rights) in enumerate(left):
-        for r in rights:
-            for at in range(r.shape[1] // width):
-                plan.append((i, len(flat), at))
-            flat.append(r)
-    steps = len(plan)
-    nl, nr = len(left), len(flat)
-    total = steps * width
-
-    def body(meta, *rest):
-        lefts, rights, rest = rest[:nl], rest[nl : nl + nr], rest[nl + nr :]
-        got = None
-        if recv is not None:
-            got, rest = rest[0], rest[1:]
-        nout = 1 if recv is None else 3
-        outs, rest = rest[:nout], rest[nout:]
-        held, sems = rest
-        step = pl.program_id(0)
-
-        @pl.when(step == 0)
-        def _():
-            copies = []
-            for i in range(nl):
-                for j in range(4):
-                    start = pl.multiple_of(meta[first + j] * BAND, BAND)
-                    copies.append(
-                        pltpu.make_async_copy(
-                            lefts[i].at[pl.ds(start, BAND)],
-                            held.at[i, pl.ds(j * BAND, BAND)],
-                            sems.at[i * 4 + j],
-                        )
-                    )
-            for copy in copies:
-                copy.start()
-            for copy in copies:
-                copy.wait()
-
-        def emit(which, right):
-            value = dot(held[which], right)
-            if recv is None:
-                outs[0][...] = value.astype(bf16)
-                return
-            low = (value + got[...].astype(f32)).astype(bf16)
-            outs[0][...] = low[:BAND]
-            outs[1][...] = low[BAND : 2 * BAND]
-            outs[2][...] = low[2 * BAND :]
-
-        begin = 0
-        for r in range(nr):
-            mine = [s for s, p in enumerate(plan) if p[1] == r]
-
-            @pl.when((step >= mine[0]) & (step <= mine[-1]))
-            def _(r=r):
-                which = plan[[s for s, p in enumerate(plan) if p[1] == r][0]][0]
-                emit(which, rights[r][...])
-
-    def right_spec(r):
-        mine = [s for s, p in enumerate(plan) if p[1] == r]
-        return pl.BlockSpec((rows, width), lambda s, m: (0, jnp.clip(s - mine[0], 0, len(mine) - 1)))
-
-    cols = lambda n: pl.BlockSpec((n, width), lambda s, m: (0, s))
-    ins = [l for l, _ in left] + flat + ([] if recv is None else [recv])
-    in_specs = [ANY] * nl + [right_spec(r) for r in range(nr)]
-    if recv is None:
-        outs, out_specs = [shape((4 * BAND, total), bf16)], [cols(4 * BAND)]
-    else:
-        in_specs.append(cols(4 * BAND))
-        outs = [shape((n * BAND, total), bf16) for n in (1, 1, 2)]
-        out_specs = [cols(n * BAND) for n in (1, 1, 2)]
+def second_grad(order, up_left, up_right, out_left, out_right):
+    rows = up_right.shape[0]
+    blocks = FF // D + 1
+
+    def body(meta, up_left, out_left, up_right, out_right, send, own, near, far, held):
+        def emit(left, right):
+            held[...] = dot(left[...], right[...]).astype(bf16)
+            for j in range(8):
+                low = held[pl.ds(pl.multiple_of(meta[5 + j] * BAND, BAND), BAND)]
+                if j < 4:
+                    send[j] = low
+                elif j < 6:
+                    (own, near)[j - 4][...] = low
+                else:
+                    far[j - 6] = low
+
+        last = pl.program_id(0) == blocks - 1
+
+        @pl.when(jnp.logical_not(last))
+        def _():
+            emit(up_left, up_right)
+
+        @pl.when(last)
+        def _():
+            emit(out_left, out_right)
+
+    many = lambda n: pl.BlockSpec((n, BAND, D), lambda s, m: (0, s, 0))
+    one = pl.BlockSpec((BAND, D), lambda s, m: (s, 0))
+    flat = (blocks * BAND, D)
     return order.run(
-        name,
+        "second_grad",
         body,
-        ins,
-        in_specs,
-        outs,
-        out_specs,
-        (steps,),
-        [pltpu.VMEM((nl, 4 * BAND, rows), bf16), pltpu.SemaphoreType.DMA((4 * nl,))],
-        rows * 4 * BAND * total,
-        24,
-    )
+        [up_left, out_left, up_right, out_right],
+        [
+            whole((D, rows)),
+            whole((D, rows)),
+            pl.BlockSpec((rows, D), lambda s, m: (0, jnp.minimum(s, blocks - 2))),
+            whole((rows, D)),
+        ],
+        [shape((4, *flat), bf16), shape(flat, bf16), shape(flat, bf16), shape((2, *flat), bf16)],
+        [many(4), one, one, many(2)],
+        (blocks,),
+        [pltpu.VMEM((D, D), bf16)],
+        rows * D * blocks * D,
+        28,
+    )
+
+
+def collect(order, first_sums, chunk_sums, mid_sums, down_sum, up_sum):
+    def body(meta, first, *refs):
+        chunks, (mid, down, up, out) = refs[:-4], refs[-4:]
+        out[...] = jnp.zeros_like(out)
+        out[0:2] = first[0:2]
+        at = 0
+        for ref in chunks:
+            w = ref.shape[1] // 3
+            out[2:3, at : at + w] = ref[0:1, :w]
+            out[3:4, at : at + w] = ref[0:1, 2 * w :]
+            at += w
+        out[4:5] = mid[2:3]
+        out[5:7] = mid[0:2]
+        out[7:8] = down[0:1]
+        for i in range(FF // D):
+            out[8 + i : 9 + i] = up[0:1, i * D : (i + 1) * D]
+
+    ins = [first_sums, *chunk_sums, mid_sums, down_sum, up_sum]
+    return order.small("collect", body, ins, [shape((16, D), f32)])[0]
 
 
 class Links:
@@ -770,15 +911,6 @@
     def far(self, value):
         return self.move(value, lambda w, n: (w, n ^ (2 - (w & 1))))
 
-    def inward(self, value):
-        return self.move(value, lambda w, n: {0: (w + 2, n), 3: (w - 2, n)}.get(w >> 1))
-
-    def across(self, value):
-        return self.move(value, lambda w, n: {1: (w + 2, n), 2: (w - 2, n)}.get(w >> 1))
-
-    def outward(self, value):
-        return self.move(value, lambda w, n: {1: (w - 2, n), 2: (w + 2, n)}.get(w >> 1))
-
     def along(self, value, step):
         return self.move(value, lambda w, n: (w, n ^ step))
 
@@ -793,11 +925,13 @@
                 a, b, d = n ^ (1 + core), n ^ (2 - core), n ^ 3
                 if not self.paired:
                     row = [0] * 5 + list(range(8)) + [0, 0] + list(range(self.narrow))
+                    row += [0] * (20 - len(row))
                 else:
                     row = [2 * n, 2 * a, 2 * d + core, 2 * b, 2 * d + 1 - core]
                     row += [2 * s + 1 - core for s in (n, a, b, d)]
                     row += [2 * s + core for s in (n, b, a, d)]
                     row += [core, int(level in (1, 2)), n, n ^ 1, n ^ 2, d]
+                    row += [2 * d]
                 table.append(row)
         place = lax.axis_index(("wide", "narrow"))
         return lax.dynamic_index_in_dim(jnp.array(table, jnp.int32), place, keepdims=False)
@@ -808,23 +942,40 @@
             return [sources[i] for i in range(self.narrow)]
         return [packed] + [self.along(packed, i) for i in (1, 2, 3)]
 
-    def sum_all(self, value):
-        if not self.paired:
-            return lax.psum(value, ("wide", "narrow"))
-        value = value + self.swap(value)
-        value = value + self.along(value, 1) + self.along(value, 2) + self.along(value, 3)
-        return value + self.level(value, 1) + self.level(value, 2) + self.level(value, 3)
-
-    def sum_levels(self, own):
-        groups = [list(range(c, self.wide, 2)) for c in range(2)]
-        return lax.psum(own, "wide", axis_index_groups=groups)
-
-    def whole_sum(self, sent, kept):
-        full = jnp.concatenate([sent, *kept], 0)
+    def inward(self, value):
+        return self.move(value, lambda w, n: {0: (w + 2, n), 3: (w - 2, n)}.get(w >> 1))
+
+    def across(self, value):
+        return self.move(value, lambda w, n: {1: (w + 2, n), 2: (w - 2, n)}.get(w >> 1))
+
+    def outward(self, value):
+        return self.move(value, lambda w, n: {1: (w - 2, n), 2: (w + 2, n)}.get(w >> 1))
+
+    def whole_sum(self, sent, own, near, far):
+        rest = own.shape[0]
+        band = rest if rest == FF // 8 else BAND
+        full = jnp.concatenate([sent, own[None], near[None], far], 0)
+        full = full.reshape(8, rest // band, band, D)
         mine = lax.psum_scatter(full, "narrow", scatter_dimension=0, tiled=True)
-        mine = lax.psum(mine, "wide")
-        half = mine.shape[0] // 2
-        return mine[:half], mine[half:]
+        mine = lax.psum(mine, "wide").transpose(1, 0, 2, 3).reshape(rest // band, -1, D)
+        half = mine.shape[1] // 2
+        return mine[:, :half].reshape(-1, D), mine[:, half:].reshape(-1, D)
+
+
+def finish_two(order, d_pair, s_pair, half):
+    blocks = FF // D
+    up, out = finish(
+        order,
+        half,
+        [s_pair],
+        [(FF, [(0, i, 0, D) for i in range(blocks)]), (D, [(0, blocks, 0, D)])],
+    )
+    (down,) = finish(order, d_pair[0].shape[0], [d_pair], [(D, [(0, 0, 0, D)])])
+    return down, up, out
+
+
+def split(got):
+    return got[:3], got[3:]
 
 
 def layer(links, *args):
@@ -865,168 +1016,159 @@
     live = segment_ids.reshape(-1, 1, TILE)
 
     pack_one = pack(order, [query_weight, key_weight, value_weight])
+    pack_two = pack(order, [up_weight, output_weight])
     shares = links.shares(jnp.concatenate([*small, up_bias]).reshape(-1, share))
     vec, up_b = vectors(order, shares)
     if paired:
         near_one = links.near(pack_one)
-        far_one = links.far(copies(order, [near_one])[0])
-        w_one = [pack_one, near_one, far_one, links.swap(near_one), links.swap(far_one)]
+        far_one = links.far(near_one)
+        w_one = [pack_one, near_one, far_one, links.swap(near_one)]
     else:
         w_one = gather(pack_one)
-    pack_two = pack(order, [up_weight, output_weight])
+    if paired:
+        order.last.append(far_one)
+        pack_two = gate(order, pack_two)
     kept = attend(order, tokens, vec, segment_ids, w_one, 0, None)
     if paired:
         near_two = links.near(pack_two)
-        far_two = links.far(copies(order, [near_two])[0])
-        w_two = [pack_two, near_two, far_two, links.swap(near_two), links.swap(far_two)]
+        half_two, down_copy = copies(order, [near_two], [down_weight])
+        far_two = links.far(half_two)
+        got_two, near_down = links.swap(near_two), links.near(down_copy)
     else:
         w_two = gather(pack_two)
     for s in range(1, tokens.shape[0] // LEN):
         kept = attend(order, tokens, vec, segment_ids, w_one, s, list(kept))
     fn_t, q, k, v, att, att_t, expo, inv = kept
     if paired:
-        down_half, down_copy = copies(order, [down_weight], [down_weight])
-        near_down = links.near(down_copy)
+        down_half, far_two = copies(order, [down_weight], [far_two])
+        w_two = [pack_two, near_two, far_two, got_two, links.swap(far_two)]
         far_down = links.along(down_half, 3)
-        w_down = [down_weight, near_down, far_down, links.swap(near_down), links.swap(far_down)]
     else:
         w_down = gather(down_weight)
     mid, sn_t, hidden, slope, gb, down_sum = feed(
         order, att, tokens, out_grad, live, vec, up_b, w_two
     )
 
+    if paired:
+        near_down, far_down = copies(order, [], [near_down, far_down])
+        w_down = [down_weight, near_down, far_down, links.swap(near_down), links.swap(far_down)]
     d_send, d_own, d_near, d_far = down_grad(order, hidden, gb)
+    if paired:
+        d_got = links.swap(d_send)
+    every, pair = ..., slice(2, 4)
+    if paired:
+        (d_far,) = sums_of(order, [[(d_far, every), (d_got, pair)]])
+        d_got2 = links.near(d_far)
     gpre, gmid, gattn, gatt, mid_sums, up_sum = back(order, slope, mid, gb, vec, w_down, w_two)
-    lefts = [(sn_t, [gpre]), (att_t, [gattn])]
-    if paired:
-        high = d_own.shape[0]
-        d_got = links.swap(d_send)
-        (d_far,) = sums_of(order, [(2 * high, [(d_far, 0), (d_got, 2 * high)])])
-        d_got2 = links.near(d_far)
-    s_send = weight_grad("second_send", order, lefts, 5, None)[0]
-    s_got = links.swap(s_send) if paired else jnp.zeros_like(s_send)
-
-    chunks, first = [], 0
-    for c, pairs in enumerate(CHUNKS):
-        chunks.append(attend_back(order, fn_t, q, k, v, att_t, gatt, expo, inv, first, pairs))
-        first += pairs
-        if c == 0:
-            if paired:
-                c_send, c_own, c_near, c_far = chunks[0][3:7]
-                d_near, d_own = sums_of(
-                    order,
-                    [
-                        (high, [(d_near, 0), (d_got, high), (d_got2, high)]),
-                        (high, [(d_own, 0), (d_got, 0), (d_got2, 0)]),
-                    ],
-                )
-                d_got3 = links.far(d_near)
-                c_got = links.swap(c_send)
-            s_own, s_near, s_far = weight_grad("second_keep", order, lefts, 9, s_got)
-            if paired:
-                s_got2 = links.near(s_far)
-                d_own, c_far = sums_of(
-                    order,
-                    [
-                        (high, [(d_own, 0), (d_got3, 0)]),
-                        (2 * BAND, [(c_far, 0), (c_got, 2 * BAND)]),
-                    ],
-                )
-                d_got = links.inward(d_own)
-                c_got2 = links.near(c_far)
-    dqkv = [chunk[:3] for chunk in chunks]
-    if paired:
-        e_send, e_own, e_near, e_far = chunks[1][3:7]
-        e_got = links.swap(e_send)
+    if paired:
+        d_near, d_own = sums_of(
+            order,
+            [[(d_near, every), (d_got, 1), (d_got2, 1)]],
+            [[(d_own, every), (d_got, 0), (d_got2, 0)]],
+        )
+        d_got = links.far(d_near)
+    s_send, s_own, s_near, s_far = second_grad(order, sn_t, gpre, att_t, gattn)
+    if paired:
+        s_got = links.swap(s_send)
+        (s_far,) = sums_of(order, [[(s_far, every), (s_got, pair)]])
+        s_got2 = links.near(s_far)
+    c_three, (c_send, c_own, c_near, c_far, c_sums) = split(
+        attend_back(order, fn_t, q, k, v, att_t, gatt, expo, inv, 0, CHUNKS[0])
+    )
+    if paired:
+        c_got = links.swap(c_send)
         s_near, s_own, d_own = sums_of(
             order,
-            [
-                (BAND, [(s_near, 0), (s_got2, BAND)]),
-                (BAND, [(s_own, 0), (s_got2, 0)]),
-                (high, [(d_own, 0), (d_got, 0)]),
-            ],
+            [[(s_near, every), (s_got, 1), (s_got2, 1)]],
+            [[(s_own, every), (s_got, 0), (s_got2, 0)]],
+            [[(d_own, every), (d_got, every)]],
         )
         s_got = links.far(s_near)
-        d_got = links.across(d_own)
-        c_near, c_own, e_far = sums_of(
+        d_got = links.inward(d_own)
+    e_three, (e_send, e_own, e_near, e_far, e_sums) = split(
+        attend_back(order, fn_t, q, k, v, att_t, gatt, expo, inv, CHUNKS[0], CHUNKS[1])
+    )
+    if paired:
+        e_got = links.swap(fetch(order, e_send)[0])
+        s_own, d_own = sums_of(
+            order, [[(s_own, every), (s_got, every)]], [[(d_own, every), (d_got, every)]]
+        )
+        s_got, d_got = links.inward(s_own), links.across(d_own)
+        (g_far,) = sums_of(
+            order, [[(c_far, every), (c_got, pair)], [(e_far, every), (e_got, pair)]]
+        )
+        g_got = links.near(g_far)
+    input_grad, first_sums = grad_first(
+        order, [c_three, e_three], tokens, gmid, vec, w_one
+    )
+    total = collect(order, first_sums, [c_sums, e_sums], mid_sums, down_sum, up_sum)
+    if paired:
+        totals = [total] + [links.along(total, i) for i in (1, 2, 3)]
+        cut = c_own.shape[0]
+        low, high = (slice(0, cut), slice(None)), (slice(cut, None), slice(None))
+        g_near, g_own, s_own, d_own = sums_of(
             order,
             [
-                (BAND, [(c_near, 0), (c_got, BAND), (c_got2, BAND)]),
-                (BAND, [(c_own, 0), (c_got, 0), (c_got2, 0)]),
-                (2 * BAND, [(e_far, 0), (e_got, 2 * BAND)]),
+                [(c_near, every), (c_got, 1), (g_got, (1, *low))],
+                [(e_near, every), (e_got, 1), (g_got, (1, *high))],
             ],
+            [
+                [(c_own, every), (c_got, 0), (g_got, (0, *low))],
+                [(e_own, every), (e_got, 0), (g_got, (0, *high))],
+            ],
+            [[(s_own, every), (s_got, every)]],
+            [[(d_own, every), (d_got, every)]],
         )
-        c_got = links.far(c_near)
-        e_got2 = links.near(e_far)
-    input_grad, first_sums = grad_first(order, dqkv, tokens, gmid, vec, w_one)
-    cols = lambda c, i: slice(i * PAIR * CHUNKS[c], (i + 1) * PAIR * CHUNKS[c])
-    bias = lambda i: jnp.concatenate([chunks[c][7][:1, cols(c, i)] for c in range(2)], 1)
-    total = links.sum_all(
-        jnp.concatenate(
-            [
-                first_sums[:2],
-                bias(0),
-                bias(2),
-                mid_sums[2:3],
-                mid_sums[:2],
-                down_sum[:1],
-                up_sum[:1].reshape(4, D),
-            ],
-            0,
+        g_got = links.far(g_near)
+        s_got, d_got = links.across(s_own), links.outward(d_own)
+    layer_out = down_out(order, hidden, mid, vec, w_down)
+    if paired:
+        g_own, s_own = sums_of(
+            order,
+            [[(g_own, every), (g_got, every)], [(t, every) for t in totals]],
+            [[(s_own, every), (s_got, every)]],
         )
-    )
-    if paired:
-        e_near, e_own, c_own, s_own, d_own = sums_of(
-            order,
-            [
-                (BAND, [(e_near, 0), (e_got, BAND), (e_got2, BAND)]),
-                (BAND, [(e_own, 0), (e_got, 0), (e_got2, 0)]),
-                (BAND, [(c_own, 0), (c_got, 0)]),
-                (BAND, [(s_own, 0), (s_got, 0)]),
-                (high, [(d_own, 0), (d_got, 0)]),
-            ],
-        )
-        e_got = links.far(e_near)
-        c_got = links.level(c_own, 1)
-        s_own = links.sum_levels(s_own)
-        d_got = links.outward(d_own)
-    layer_out = down_out(order, hidden, mid, vec, w_down)
-    if paired:
-        e_own, c_own = sums_of(
-            order,
-            [(BAND, [(e_own, 0), (e_got, 0)]), (BAND, [(c_own, 0), (c_got, 0)])],
-        )
-        e_got, c_got = links.level(e_own, 1), links.level(c_own, 2)
+        g_got, s_got = links.inward(g_own), links.outward(s_own)
         d_own = pick(order, d_own, d_got)
         d_pair = (d_own, links.swap(d_own))
-        e_own, c_own = sums_of(
-            order,
-            [(BAND, [(e_own, 0), (e_got, 0)]), (BAND, [(c_own, 0), (c_got, 0)])],
-        )
-        e_got = links.level(e_own, 2)
-        c_pair = (c_own, links.swap(c_own))
+        (g_own,) = sums_of(order, [[(g_own, every), (g_got, every)]])
+        g_got = links.across(g_own)
+        s_own = pick(order, s_own, s_got)
         s_pair = (s_own, links.swap(s_own))
-        (down_weight_grad,) = finish(order, [d_pair], [(D, [(0, 0, D)])])
-        (e_own,) = sums_of(order, [(BAND, [(e_own, 0), (e_got, 0)])])
-        e_pair = (e_own, links.swap(e_own))
+        (g_own,) = sums_of(order, [[(g_own, every), (g_got, every)]])
+        g_got = links.outward(g_own)
+        finished = finish_two(order, d_pair, s_pair, share // 2)
+        g_own = pick(order, g_own, g_got)
+        g_pair = (g_own, links.swap(g_own))
     else:
-        d_pair = links.whole_sum(d_send, (d_own, d_near, d_far))
-        s_pair = links.whole_sum(s_send, (s_own, s_near, s_far))
-        c_pair, e_pair = [links.whole_sum(c[3], c[4:7]) for c in chunks]
-        (down_weight_grad,) = finish(order, [d_pair], [(D, [(0, 0, D)])])
-    first_grads = finish(
-        order,
-        [c_pair, e_pair],
-        [(D, [(c, cols(c, i).start, PAIR * CHUNKS[c]) for c in range(2)]) for i in range(3)],
-    )
-    up_weight_grad, output_weight_grad = finish(
-        order, [s_pair], [(FF, [(0, 0, FF)]), (D, [(0, FF, D)])]
-    )
+        s_pair = links.whole_sum(s_send, s_own, s_near, s_far)
+        d_pair = links.whole_sum(d_send, d_own, d_near, d_far)
+        c_pair = links.whole_sum(c_send, c_own, c_near, c_far)
+        e_pair = links.whole_sum(e_send, e_own, e_near, e_far)
+        g_pair = [jnp.concatenate([c, e], 0) for c, e in zip(c_pair, e_pair)]
+        total = lax.psum(total, ("wide", "narrow"))
+        finished = finish_two(order, d_pair, s_pair, share // 2)
+    down_weight_grad, up_weight_grad, output_weight_grad = finished
+    half = share // 2
+    plan = []
+    for i in range(3):
+        parts = []
+        for c, pairs in enumerate(CHUNKS):
+            at, stop = i * PAIR * pairs, (i + 1) * PAIR * pairs
+            while at < stop:
+                end = min(stop, (at // D + 1) * D)
+                block = at // D + c * (3 * PAIR * CHUNKS[0] // D)
+                parts.append((0, block, at % D, end - at))
+                at = end
+        plan.append((D, parts))
+    first_grads = finish(order, half, [g_pair], plan, 16 if paired else 0)
+    if paired:
+        total = first_grads[3]
 
     n = lax.axis_index("narrow")
     mine = lax.dynamic_slice_in_dim(total[:8], n * share, share, 1)
     up_share = up_bias.shape[0]
-    up_mine = lax.dynamic_slice_in_dim(total[8:].reshape(FF), n * up_share, up_share)
+    up_mine = lax.dynamic_slice_in_dim(total[8:12].reshape(FF), n * up_share, up_share)
     return (
         layer_out,
         input_grad,

time: 380 us -> 317 us (0.83)
  local copies, waits for them, and re-layouts: 43.3 us -> 5.69 us
  waiting for transfers between devices: 98.1 us -> 72.6 us
  between operations: 14.8 us -> 1.29 us
  Pallas kernels: 179 us -> 187 us
  starting transfers between devices: 43.1 us -> 48.5 us
    unnamed x126 -> x30, local copies, waits for them, and re-layouts: 33.3 us -> 3.41 us
    ppermute x45 -> x39, waiting for transfers between devices: 92.1 us -> 72.6 us  [move(): return lax.ppermute(value, ('wide', 'narrow'), pairs)]
    pallas_call x19 -> x21, Pallas kernels: 15.3 us -> 28.8 us  [small(): pl.pallas_call(inner, out_shape=outs, in_specs=[pl.BlockSpec(memory_space...]
    slice x8 -> x1, local copies, waits for them, and re-layouts: 7.11 us -> 0.01 us  [layer(): total[8:12].reshape(FF)]
    psum x1 -> x0, waiting for transfers between devices: 5.95 us -> none  [sum_levels(): return lax.psum(own, 'wide', axis_index_groups=groups)]
    ppermute x45 -> x39, starting transfers between devices: 43 us -> 48.5 us  [move(): return lax.ppermute(value, ('wide', 'narrow'), pairs)]
    pallas_call x11 -> x14, Pallas kernels: 163 us -> 158 us  [run(): pl.pallas_call(inner, out_shape=outs, grid_spec=pltpu.PrefetchScalarGridS...]
  transfers between devices with their start and end apart: 46 -> 39, of which waited for: 13 -> 16; matrix products, arithmetic and copies ran while one was open for 3% -> 0% of each run, Pallas kernels for 43% -> 47%
where the time goes in v2:
time: 317 us; the launch traced here: 315 us
  Pallas kernels  187 us (59%)
  waiting for transfers between devices  72.6 us (23%)
  starting transfers between devices  48.5 us (15%)
  local copies, waits for them, and re-layouts  5.69 us (2%)
    pallas_call x14, Pallas kernels, run(): pl.pallas_call(inner, out_shape=outs, grid_spec=pltpu.PrefetchScalarGridS...  158 us
    ppermute x39, waiting for transfers between devices, move(): return lax.ppermute(value, ('wide', 'narrow'), pairs)  72.6 us
    ppermute x39, starting transfers between devices, move(): return lax.ppermute(value, ('wide', 'narrow'), pairs)  48.5 us
    pallas_call x21, Pallas kernels, small(): pl.pallas_call(inner, out_shape=outs, in_specs=[pl.BlockSpec(memory_space...  28.8 us
  transfers between devices with their start and end apart: 39, of which 16 were waited for; matrix products, arithmetic and copies ran while one was open for 0% of the time, Pallas kernels for 47%

profile of v2, /device:TPU:0, one launch (start us, length us, event | category | flops | bytes accessed | tf_op | source)
XLA Modules:
  0.0 315.3 jit_solution(11674782602256109801)
XLA Ops:
  3.2 3.0 collective-permute-start.3
  6.2 11.0 %collective-permute-done.3.refs_4_.refs_10_ = bf16[192,2304]{1,0:T(8,128)(2,1)S(1)} collective-permute-done((bf16[192,2304]{1,0:T(8,128)(2,1)S(1)}, bf16[192,2304]{1,0:T(8,128)(2,1)S(1)}, u32[]{:S(2)}, u32[]{:S(2)}) %collective-permute-start.3) | collective-permute-done | bytes 884768 | tf_op jit(solution)/shard_map/ppermute | solution.py:903
  24.9 5.7 %collective-permute-done.1.refs_2_ = bf16[12,192]{1,0:T(8,128)(2,1)S(1)} collective-permute-done((bf16[12,192]{1,0:T(8,128)(2,1)S(1)}, bf16[12,192]{1,0:T(8,128)(2,1)S(1)}, u32[]{:S(2)}, u32[]{:S(2)}) %collective-permute-start.1) | collective-permute-done | bytes 4640 | tf_op jit(solution)/shard_map/ppermute | solution.py:903
  33.9 2.4 collective-permute-done.5.refs_6_.refs_12_
  36.3 14.2 %attend.2 = (bf16[768,1024]{1,0:T(8,128)(2,1)}, bf16[1024,768]{1,0:T(8,128)(2,1)}, bf16[1024,768]{1,0:T(8,128)(2,1)}, bf16[1024,768]{1,0:T(8,128)(2,1)}, bf16[10...) custom-call(s32[20]{0:T(128)S(1)} %dynamic-slice_bitcast_fusion.meta, ...), custom_call_target="tpu_custom_call" | custom-call | flops 1 | bytes 400000000 | tf_op jit(solution)/shard_map/attend/pallas_call | solution.py:84
  55.5 14.4 %attend.3 = (bf16[768,1024]{1,0:T(8,128)(2,1)}, bf16[1024,768]{1,0:T(8,128)(2,1)}, bf16[1024,768]{1,0:T(8,128)(2,1)}, bf16[1024,768]{1,0:T(8,128)(2,1)}, bf16[10...) custom-call(s32[20]{0:T(128)S(1)} %dynamic-slice_bitcast_fusion.meta, ...), custom_call_target="tpu_custom_call", output_to_operand_aliasing={{0}: (8, {}), {1}: (9, {}), {2}: (10, {}), {3}: (11, {}), {... | custom-call | flops 1 | bytes 400000000 | tf_op jit(solution)/shard_map/attend/pallas_call | solution.py:84
  71.6 3.4 %collective-permute-start.11 = (bf16[384,768]{1,0:T(8,128)(2,1)S(1)}, bf16[384,768]{1,0:T(8,128)(2,1)S(1)}, u32[]{:S(2)}, u32[]{:S(2)}) collective-permute-start(bf16[384,768]{1,0:T(8,128)(2,1)S(1)} %get-tuple-element.112.refs_11_), channel_id=1, source_target_pairs={{0,3},{1,2},{2,1},{3,0},{4,7},{5,6},{6,5},{7,4},{8,11},{9,10},{10,... | collective-permute-start | bytes 1769480 | tf_op jit(solution)/shard_map/ppermute | solution.py:903
  75.0 22.2 %feed.1 = (f32[1024,768]{1,0:T(8,128)}, bf16[768,1024]{1,0:T(8,128)(2,1)}, bf16[1024,3072]{1,0:T(8,128)(2,1)}, bf16[1024,3072]{1,0:T(8,128)(2,1)}, bf16[1024,768]{1,0:T(8,128)(2,1)}, /*index=5*/f32[8,768]{1,0:T(8,128)}) custom-call(s32[20]{0:T(128)S(1)} %dynamic-slice_bitcast_fusion.meta, bf16[1024,768]{1,0:T(8,128)(2,1)} %get-tuple-element.108.refs_0_, ...), custom_call_target="tpu_custom_call" | custom-call | flops 1 | bytes 400000000 | tf_op jit(solution)/shard_map/feed/pallas_call | solution.py:84
  97.9 12.3 %down_grad.1 = (bf16[4,384,768]{2,1,0:T(8,128)(2,1)}, bf16[384,768]{1,0:T(8,128)(2,1)}, bf16[384,768]{1,0:T(8,128)(2,1)}, bf16[2,384,768]{2,1,0:T(8,128)(2,1)}) custom-call(s32[20]{0:T(128)S(1)} %dynamic-slice_bitcast_fusion.meta, bf16[1024,3072]{1,0:T(8,128)(2,1)} %get-tuple-element.113.refs_0_, bf16[1024,768]{1,0:T(8,128)(2,1)} %get-tuple-element.123.refs_1_.refs_2_, ...), custom_call_target="tpu_custom_call" | custom-call | flops 1 | bytes 400000000 | tf_op jit(solution)/shard_map/down_grad/pallas_call | solution.py:84
  110.7 5.9 %collective-permute-done.14.refs_1_ = bf16[4,384,768]{2,1,0:T(8,128)(2,1)S(1)} collective-permute-done((bf16[4,384,768]{2,1,0:T(8,128)(2,1)}, bf16[4,384,768]{2,1,0:T(8,128)(2,1)S(1)}, u32[]{:S(2)}, u32[]{:S(2)}) %collective-permute-start.14) | collective-permute-done | bytes 2359328 | tf_op jit(solution)/shard_map/ppermute | solution.py:903
  121.6 23.6 %back.1 = (bf16[1024,3072]{1,0:T(8,128)(2,1)}, f32[1024,768]{1,0:T(8,128)}, bf16[1024,768]{1,0:T(8,128)(2,1)}, bf16[1024,768]{1,0:T(8,128)(2,1)}, f32[8,768]{1,0:T(8,128)}, /*index=5*/f32[8,3072]{1,0:T(8,128)}) custom-call(s32[20]{0:T(128)S(1)} %dynamic-slice_bitcast_fusion.meta, bf16[1024,3072]{1,0:T(8,128)(2,1)} %get-tuple-element.122.refs_0_, ...), custom_call_target="tpu_custom_call" | custom-call | flops 1 | bytes 400000000 | tf_op jit(solution)/shard_map/back/pallas_call | solution.py:84
  147.4 12.4 %second_grad.1 = (bf16[4,480,768]{2,1,0:T(8,128)(2,1)}, bf16[480,768]{1,0:T(8,128)(2,1)}, bf16[480,768]{1,0:T(8,128)(2,1)}, bf16[2,480,768]{2,1,0:T(8,128)(2,1)}) custom-call(s32[20]{0:T(128)S(1)} %dynamic-slice_bitcast_fusion.meta, bf16[768,1024]{1,0:T(8,128)(2,1)} %get-tuple-element.129.refs_0_, bf16[768,1024]{1,0:T(8,128)(2,1)} %get-tuple-element.121.refs_1_.refs_3_, ...), custom_call_target="tpu_custom_call" | custom-call | flops 1 | bytes 400000000 | tf_op jit(solution)/shard_map/second_grad/pallas_call | solution.py:84
  160.2 5.2 %collective-permute-done.16.refs_1_ = bf16[4,480,768]{2,1,0:T(8,128)(2,1)S(1)} collective-permute-done((bf16[4,480,768]{2,1,0:T(8,128)(2,1)}, bf16[4,480,768]{2,1,0:T(8,128)(2,1)S(1)}, u32[]{:S(2)}, u32[]{:S(2)}) %collective-permute-start.16) | collective-permute-done | bytes 2949152 | tf_op jit(solution)/shard_map/ppermute | solution.py:903
  170.3 20.7 %attend_back.2 = (bf16[1024,512]{1,0:T(8,128)(2,1)}, bf16[1024,512]{1,0:T(8,128)(2,1)}, bf16[1024,512]{1,0:T(8,128)(2,1)}, bf16[4,192,768]{2,1,0:T(8,128)(2,1)},...) custom-call(s32[20]{0:T(128)S(1)} %dynamic-slice_bitcast_fusion.meta, ...), custom_call_target="tpu_custom_call" | custom-call | flops 1 | bytes 400000000 | tf_op jit(solution)/shard_map/attend_back/pallas_call | solution.py:84
  193.4 2.6 sums_of.13
  197.3 3.5 %collective-permute-start.22 = (bf16[384,768]{1,0:T(8,128)(2,1)S(1)}, bf16[384,768]{1,0:T(8,128)(2,1)S(1)}, u32[]{:S(2)}, u32[]{:S(2)}) collective-permute-start(bf16[384,768]{1,0:T(8,128)(2,1)S(1)} %get-tuple-element.149.refs_2_), channel_id=1, source_target_pairs={{0,8},{1,9},{2,10},{3,11},{4,12},{5,13},{6,14},{7,15},{24,16},{25,... | collective-permute-start | bytes 1769480 | tf_op jit(solution)/shard_map/ppermute | solution.py:903
  200.8 12.8 %attend_back.3 = (bf16[1024,256]{1,0:T(8,128)(2,1)}, bf16[1024,256]{1,0:T(8,128)(2,1)}, bf16[1024,256]{1,0:T(8,128)(2,1)}, bf16[4,96,768]{2,1,0:T(8,128)(2,1)}, ...) custom-call(s32[20]{0:T(128)S(1)} %dynamic-slice_bitcast_fusion.meta, ...), custom_call_target="tpu_custom_call" | custom-call | flops 1 | bytes 400000000 | tf_op jit(solution)/shard_map/attend_back/pallas_call | solution.py:84
  222.6 10.2 %grad_first.1 = (bf16[1024,768]{1,0:T(8,128)(2,1)}, f32[8,768]{1,0:T(8,128)}) custom-call(s32[20]{0:T(128)S(1)} %dynamic-slice_bitcast_fusion.meta, bf16[1024,768]{1,0:T(8,128)(2,1)} %refs_0_.11, f32[1024,768]{1,0:T(8,128)} %get-tuple-element.155.refs_1_, f32[8,768]{1,0:T(8,128)} %copy-done.4, bf16[1024,512]{1,0:T(8,128)(2,1)} %get-tuple-element.143.refs_6_.refs_3_, ...), custom_call_target="tpu_custom_call" | custom-call | flops 1 | bytes 400000000 | tf_op jit(solution)/shard_map/grad_first/pallas_call | solution.py:84
  234.4 2.9 collective-permute-done.24.refs_8_
  247.8 10.0 %down_out.1.refs_8_ = bf16[1024,768]{1,0:T(8,128)(2,1)} custom-call(s32[20]{0:T(128)S(1)} %dynamic-slice_bitcast_fusion.meta, bf16[1024,3072]{1,0:T(8,128)(2,1)} %get-tuple-element.113.refs_0_, f32[1024,768]{1,0:T(8,128)} %get-tuple-element.114.refs_2_.refs_1_, f32[8,768]{1,0:T(8,128)} %copy-done.4, bf16[768,768]{1,0:T(8,128)(2,1)S(1)} %copy-done.1, ...), custom_call_target="tpu_custom_call" | custom-call | flops 1 | bytes 400000000 | tf_op jit(solution)/shard_map/down_out/pallas_call | solution.py:84
  259.9 7.3 %collective-permute-start.31 = (bf16[304,768]{1,0:T(8,128)(2,1)S(1)}, bf16[304,768]{1,0:T(8,128)(2,1)S(1)}, u32[]{:S(2)}, u32[]{:S(2)}) collective-permute-start(bf16[304,768]{1,0:T(8,128)(2,1)S(1)} %get-tuple-element.170.refs_2_.refs_0_), channel_id=1, source_target_pairs={{0,8},{1,9},{2,10},{3,11},{4,12},{5,13},{6,14},{7,15},{24,16},{25,... | collective-permute-start | bytes 1400840 | tf_op jit(solution)/shard_map/ppermute | solution.py:903
  267.9 10.1 %collective-permute-done.31.refs_1_ = bf16[304,768]{1,0:T(8,128)(2,1)S(1)} collective-permute-done((bf16[304,768]{1,0:T(8,128)(2,1)S(1)}, bf16[304,768]{1,0:T(8,128)(2,1)S(1)}, u32[]{:S(2)}, u32[]{:S(2)}) %collective-permute-start.31) | collective-permute-done | bytes 466976 | tf_op jit(solution)/shard_map/ppermute | solution.py:903
  279.3 3.4 %collective-permute-done.34.refs_1_ = bf16[480,768]{1,0:T(8,128)(2,1)S(1)} collective-permute-done((bf16[480,768]{1,0:T(8,128)(2,1)S(1)}, bf16[480,768]{1,0:T(8,128)(2,1)S(1)}, u32[]{:S(2)}, u32[]{:S(2)}) %collective-permute-start.34) | collective-permute-done | bytes 737312 | tf_op jit(solution)/shard_map/ppermute | solution.py:903
  291.9 16.0 %collective-permute-done.35.refs_1_ = bf16[304,768]{1,0:T(8,128)(2,1)S(1)} collective-permute-done((bf16[304,768]{1,0:T(8,128)(2,1)S(1)}, bf16[304,768]{1,0:T(8,128)(2,1)S(1)}, u32[]{:S(2)}, u32[]{:S(2)}) %collective-permute-start.35) | collective-permute-done | bytes 466976 | tf_op jit(solution)/shard_map/ppermute | solution.py:903
  (127 shorter events, 78.9 us)
Async XLA Ops:
  3.2 14.0 %collective-permute-start.3 = (bf16[192,2304]{1,0:T(8,128)(2,1)S(1)}, bf16[192,2304]{1,0:T(8,128)(2,1)S(1)}, u32[]{:S(2)}, u32[]{:S(2)}) collective-permute-start(bf16[192,2304]{1,0:T(8,128)(2,1)S(1)} %pack.2.refs_2_.refs_3_.refs_9_), channel_id=1, source_target_pairs={{0,1},{1,0},{2,3},{3,2},{4,6},{5,7},{6,4},{7,5},{8,9},{9,8},{10,11... | collective-permute-start | bytes 2654216 | tf_op jit(solution)/shard_map/ppermute | solution.py:903
  17.2 14.1 %collective-permute-start.4 = (bf16[192,2304]{1,0:T(8,128)(2,1)S(1)}, bf16[192,2304]{1,0:T(8,128)(2,1)S(1)}, u32[]{:S(2)}, u32[]{:S(2)}) collective-permute-start(bf16[192,2304]{1,0:T(8,128)(2,1)S(1)} %collective-permute-done.3.refs_4_.refs_10_), channel_id=1, source_target_pairs={{0,2},{1,3},{2,0},{3,1},{4,5},{5,4},{6,7},{7,6},{8,10},{9,11},{10,... | collective-permute-start | bytes 2654216 | tf_op jit(solution)/shard_map/ppermute | solution.py:903
  31.9 19.4 %collective-permute-start.6 = (bf16[192,3840]{1,0:T(8,128)(2,1)S(1)}, bf16[192,3840]{1,0:T(8,128)(2,1)S(1)}, u32[]{:S(2)}, u32[]{:S(2)}) collective-permute-start(bf16[192,3840]{1,0:T(8,128)(2,1)S(1)} %gate.1.refs_7_.refs_6_.refs_9_), channel_id=1, source_target_pairs={{0,1},{1,0},{2,3},{3,2},{4,6},{5,7},{6,4},{7,5},{8,9},{9,8},{10,11... | collective-permute-start | bytes 4423688 | tf_op jit(solution)/shard_map/ppermute | solution.py:903
  52.0 18.9 %collective-permute-start.7 = (bf16[96,3840]{1,0:T(8,128)(2,1)S(1)}, bf16[96,3840]{1,0:T(8,128)(2,1)S(1)}, u32[]{:S(2)}, u32[]{:S(2)}) collective-permute-start(bf16[96,3840]{1,0:T(8,128)(2,1)S(1)} %get-tuple-element.107.refs_15_), channel_id=1, source_target_pairs={{0,2},{1,3},{2,0},{3,1},{4,5},{5,4},{6,7},{7,6},{8,10},{9,11},{10,... | collective-permute-start | bytes 2211848 | tf_op jit(solution)/shard_map/ppermute | solution.py:903
  54.0 21.0 %collective-permute-start.8 = (bf16[192,3840]{1,0:T(8,128)(2,1)S(1)}, bf16[192,3840]{1,0:T(8,128)(2,1)S(1)}, u32[]{:S(2)}, u32[]{:S(2)}) collective-permute-start(bf16[192,3840]{1,0:T(8,128)(2,1)S(1)} %collective-permute-done.6.refs_0_.refs_7_.refs_10_), channel_id=1, source_target_pairs={{0,4},{1,5},{2,6},{3,7},{4,0},{5,1},{6,2},{7,3},{8,12},{9,13},{10,... | collective-permute-start | bytes 4423688 | tf_op jit(solution)/shard_map/ppermute | solution.py:903
  54.0 43.2 %collective-permute-start.10 = (bf16[768,768]{1,0:T(8,128)(2,1)S(1)}, bf16[768,768]{1,0:T(8,128)(2,1)S(1)}, u32[]{:S(2)}, u32[]{:S(2)}) collective-permute-start(bf16[768,768]{1,0:T(8,128)(2,1)S(1)} %get-tuple-element.115), channel_id=1, source_target_pairs={{0,1},{1,0},{2,3},{3,2},{4,6},{5,7},{6,4},{7,5},{8,9},{9,8},{10,11... | collective-permute-start | bytes 3538952 | tf_op jit(solution)/shard_map/ppermute | solution.py:903
  71.6 25.6 %collective-permute-start.11 = (bf16[384,768]{1,0:T(8,128)(2,1)S(1)}, bf16[384,768]{1,0:T(8,128)(2,1)S(1)}, u32[]{:S(2)}, u32[]{:S(2)}) collective-permute-start(bf16[384,768]{1,0:T(8,128)(2,1)S(1)} %get-tuple-element.112.refs_11_), channel_id=1, source_target_pairs={{0,3},{1,2},{2,1},{3,0},{4,7},{5,6},{6,5},{7,4},{8,11},{9,10},{10,... | collective-permute-start | bytes 1769480 | tf_op jit(solution)/shard_map/ppermute | solution.py:903
  118.7 26.4 %collective-permute-start.15 = (bf16[2,384,768]{2,1,0:T(8,128)(2,1)S(1)}, bf16[2,384,768]{2,1,0:T(8,128)(2,1)S(1)}, u32[]{:S(2)}, u32[]{:S(2)}) collective-permute-start(bf16[2,384,768]{2,1,0:T(8,128)(2,1)S(1)} %sums_of.10.refs_14_), channel_id=1, source_target_pairs={{0,1},{1,0},{2,3},{3,2},{4,6},{5,7},{6,4},{7,5},{8,9},{9,8},{10,11... | collective-permute-start | bytes 3538952 | tf_op jit(solution)/shard_map/ppermute | solution.py:903
  167.7 25.7 %collective-permute-start.18 = (bf16[2,480,768]{2,1,0:T(8,128)(2,1)S(1)}, bf16[2,480,768]{2,1,0:T(8,128)(2,1)S(1)}, u32[]{:S(2)}, u32[]{:S(2)}) collective-permute-start(bf16[2,480,768]{2,1,0:T(8,128)(2,1)S(1)} %sums_of.12.refs_8_), channel_id=1, source_target_pairs={{0,1},{1,0},{2,3},{3,2},{4,6},{5,7},{6,4},{7,5},{8,9},{9,8},{10,11... | collective-permute-start | bytes 4423688 | tf_op jit(solution)/shard_map/ppermute | solution.py:903
  169.2 21.8 %collective-permute-start.19 = (bf16[384,768]{1,0:T(8,128)(2,1)S(1)}, bf16[384,768]{1,0:T(8,128)(2,1)S(1)}, u32[]{:S(2)}, u32[]{:S(2)}) collective-permute-start(bf16[384,768]{1,0:T(8,128)(2,1)S(1)} %get-tuple-element.134.refs_4_), channel_id=1, source_target_pairs={{0,2},{1,3},{2,0},{3,1},{4,5},{5,4},{6,7},{7,6},{8,10},{9,11},{10,... | collective-permute-start | bytes 1769480 | tf_op jit(solution)/shard_map/ppermute | solution.py:903
  191.0 25.2 %collective-permute-start.17 = (bf16[4,192,768]{2,1,0:T(8,128)(2,1)}, bf16[4,192,768]{2,1,0:T(8,128)(2,1)S(1)}, u32[]{:S(2)}, u32[]{:S(2)}) collective-permute-start(bf16[4,192,768]{2,1,0:T(8,128)(2,1)} %get-tuple-element.138), channel_id=1, source_target_pairs={{0,4},{1,5},{2,6},{3,7},{4,0},{5,1},{6,2},{7,3},{8,12},{9,13},{10,... | collective-permute-start | bytes 3538952 | tf_op jit(solution)/shard_map/ppermute | solution.py:903
  196.0 19.3 %collective-permute-start.21 = (bf16[480,768]{1,0:T(8,128)(2,1)S(1)}, bf16[480,768]{1,0:T(8,128)(2,1)S(1)}, u32[]{:S(2)}, u32[]{:S(2)}) collective-permute-start(bf16[480,768]{1,0:T(8,128)(2,1)S(1)} %get-tuple-element.144.refs_8_), channel_id=1, source_target_pairs={{0,2},{1,3},{2,0},{3,1},{4,5},{5,4},{6,7},{7,6},{8,10},{9,11},{10,... | collective-permute-start | bytes 2211848 | tf_op jit(solution)/shard_map/ppermute | solution.py:903
  197.3 17.9 %collective-permute-start.22 = (bf16[384,768]{1,0:T(8,128)(2,1)S(1)}, bf16[384,768]{1,0:T(8,128)(2,1)S(1)}, u32[]{:S(2)}, u32[]{:S(2)}) collective-permute-start(bf16[384,768]{1,0:T(8,128)(2,1)S(1)} %get-tuple-element.149.refs_2_), channel_id=1, source_target_pairs={{0,8},{1,9},{2,10},{3,11},{4,12},{5,13},{6,14},{7,15},{24,16},{25,... | collective-permute-start | bytes 1769480 | tf_op jit(solution)/shard_map/ppermute | solution.py:903
  219.2 18.2 %collective-permute-start.23 = (bf16[2,288,768]{2,1,0:T(8,128)(2,1)S(1)}, bf16[2,288,768]{2,1,0:T(8,128)(2,1)S(1)}, u32[]{:S(2)}, u32[]{:S(2)}) collective-permute-start(bf16[2,288,768]{2,1,0:T(8,128)(2,1)S(1)} %sums_of.15.refs_13_), channel_id=1, source_target_pairs={{0,1},{1,0},{2,3},{3,2},{4,6},{5,7},{6,4},{7,5},{8,9},{9,8},{10,11... | collective-permute-start | bytes 2654216 | tf_op jit(solution)/shard_map/ppermute | solution.py:903
  220.6 16.8 %collective-permute-start.24 = (bf16[480,768]{1,0:T(8,128)(2,1)S(1)}, bf16[480,768]{1,0:T(8,128)(2,1)S(1)}, u32[]{:S(2)}, u32[]{:S(2)}) collective-permute-start(bf16[480,768]{1,0:T(8,128)(2,1)S(1)} %get-tuple-element.150.refs_4_.refs_7_), channel_id=1, source_target_pairs={{0,8},{1,9},{2,10},{3,11},{4,12},{5,13},{6,14},{7,15},{24,16},{25,... | collective-permute-start | bytes 2211848 | tf_op jit(solution)/shard_map/ppermute | solution.py:903
  221.9 12.5 %collective-permute-start.25 = (bf16[384,768]{1,0:T(8,128)(2,1)S(1)}, bf16[384,768]{1,0:T(8,128)(2,1)S(1)}, u32[]{:S(2)}, u32[]{:S(2)}) collective-permute-start(bf16[384,768]{1,0:T(8,128)(2,1)S(1)} %get-tuple-element.154.refs_9_), channel_id=1, source_target_pairs={{8,16},{9,17},{10,18},{11,19},{12,20},{13,21},{14,22},{15,23},{16,... | collective-permute-start | bytes 1769480 | tf_op jit(solution)/shard_map/ppermute | solution.py:903
  239.8 18.1 %collective-permute-start.30 = (bf16[480,768]{1,0:T(8,128)(2,1)S(1)}, bf16[480,768]{1,0:T(8,128)(2,1)S(1)}, u32[]{:S(2)}, u32[]{:S(2)}) collective-permute-start(bf16[480,768]{1,0:T(8,128)(2,1)S(1)} %get-tuple-element.169.refs_6_), channel_id=1, source_target_pairs={{8,16},{9,17},{10,18},{11,19},{12,20},{13,21},{14,22},{15,23},{16,... | collective-permute-start | bytes 2211848 | tf_op jit(solution)/shard_map/ppermute | solution.py:903
  240.5 17.3 %collective-permute-start.26 = (bf16[288,768]{1,0:T(8,128)(2,1)S(1)}, bf16[288,768]{1,0:T(8,128)(2,1)S(1)}, u32[]{:S(2)}, u32[]{:S(2)}) collective-permute-start(bf16[288,768]{1,0:T(8,128)(2,1)S(1)} %get-tuple-element.167.refs_8_), channel_id=1, source_target_pairs={{0,2},{1,3},{2,0},{3,1},{4,5},{5,4},{6,7},{7,6},{8,10},{9,11},{10,... | collective-permute-start | bytes 1327112 | tf_op jit(solution)/shard_map/ppermute | solution.py:903
  243.1 14.7 %collective-permute-start.28 = (f32[16,768]{1,0:T(8,128)S(1)}, f32[16,768]{1,0:T(8,128)S(1)}, u32[]{:S(2)}, u32[]{:S(2)}) collective-permute-start(f32[16,768]{1,0:T(8,128)S(1)} %collect.1.refs_11_.refs_2_), channel_id=1, source_target_pairs={{0,2},{1,3},{2,0},{3,1},{4,6},{5,7},{6,4},{7,5},{8,10},{9,11},{10,... | collective-permute-start | bytes 147464 | tf_op jit(solution)/shard_map/ppermute | solution.py:903
  244.0 13.8 %collective-permute-start.29 = (f32[16,768]{1,0:T(8,128)S(1)}, f32[16,768]{1,0:T(8,128)S(1)}, u32[]{:S(2)}, u32[]{:S(2)}) collective-permute-start(f32[16,768]{1,0:T(8,128)S(1)} %collect.1.refs_11_.refs_2_), channel_id=1, source_target_pairs={{0,3},{1,2},{2,1},{3,0},{4,7},{5,6},{6,5},{7,4},{8,11},{9,10},{10,... | collective-permute-start | bytes 147464 | tf_op jit(solution)/shard_map/ppermute | solution.py:903
  246.5 20.8 %collective-permute-start.32 = (bf16[384,768]{1,0:T(8,128)(2,1)S(1)}, bf16[384,768]{1,0:T(8,128)(2,1)S(1)}, u32[]{:S(2)}, u32[]{:S(2)}) collective-permute-start(bf16[384,768]{1,0:T(8,128)(2,1)S(1)} %get-tuple-element.171.refs_0_), channel_id=1, source_target_pairs={{8,0},{9,1},{10,2},{11,3},{12,4},{13,5},{14,6},{15,7},{16,24},{17,... | collective-permute-start | bytes 1769480 | tf_op jit(solution)/shard_map/ppermute | solution.py:903
  258.6 24.0 %collective-permute-start.34 = (bf16[480,768]{1,0:T(8,128)(2,1)S(1)}, bf16[480,768]{1,0:T(8,128)(2,1)S(1)}, u32[]{:S(2)}, u32[]{:S(2)}) collective-permute-start(bf16[480,768]{1,0:T(8,128)(2,1)S(1)} %get-tuple-element.172.refs_0_), channel_id=1, source_target_pairs={{8,0},{9,1},{10,2},{11,3},{12,4},{13,5},{14,6},{15,7},{16,24},{17,... | collective-permute-start | bytes 2211848 | tf_op jit(solution)/shard_map/ppermute | solution.py:903
  259.9 18.0 %collective-permute-start.31 = (bf16[304,768]{1,0:T(8,128)(2,1)S(1)}, bf16[304,768]{1,0:T(8,128)(2,1)S(1)}, u32[]{:S(2)}, u32[]{:S(2)}) collective-permute-start(bf16[304,768]{1,0:T(8,128)(2,1)S(1)} %get-tuple-element.170.refs_2_.refs_0_), channel_id=1, source_target_pairs={{0,8},{1,9},{2,10},{3,11},{4,12},{5,13},{6,14},{7,15},{24,16},{25,... | collective-permute-start | bytes 1400840 | tf_op jit(solution)/shard_map/ppermute | solution.py:903
  284.5 23.4 %collective-permute-start.35 = (bf16[304,768]{1,0:T(8,128)(2,1)S(1)}, bf16[304,768]{1,0:T(8,128)(2,1)S(1)}, u32[]{:S(2)}, u32[]{:S(2)}) collective-permute-start(bf16[304,768]{1,0:T(8,128)(2,1)S(1)} %sums_of.19.refs_2_.refs_0_), channel_id=1, source_target_pairs={{8,0},{9,1},{10,2},{11,3},{12,4},{13,5},{14,6},{15,7},{16,24},{17,... | collective-permute-start | bytes 1400840 | tf_op jit(solution)/shard_map/ppermute | solution.py:903
  (30 other events, 268.4 us)
